TPU v7x, 128 devices: a whole 4x4x4 slice. The times are simulated.
128 devices in a mesh: dp: 16 (over x, y), seq: 8 (over z, core).
Axes of the slice: x: 4, y: 4, z: 4, core: 2. Of those that a mesh axis runs over, the one named last changes fastest.
Arguments:
- tokens: bfloat16 [16384, 4096], P(('dp', 'seq')), may hold values from -6 to 6
- norm_gain: float32 [4096], replicated, may hold values from 0.1 to 1.9
- send_order: int32 [128, 128], P(('dp', 'seq')), may hold values from 0 to 127, each once within a row
- segment_ids: int32 [16, 1024], P('dp'), may hold values from 0 to 7, never falling along the last dimension, each value on 1 to 512 neighbouring positions
- w_query: bfloat16 [4096, 4096], P('dp', 'seq'), as said below
- w_key: bfloat16 [4096, 512], P('dp'), as said below
- w_value: bfloat16 [4096, 512], P('dp'), may hold values from -0.09375 to 0.09375
- w_out: bfloat16 [4096, 4096], P('seq', 'dp'), may hold values from -0.09375 to 0.09375
Outputs:
- attended: bfloat16 [16384, 4096], P(('dp', 'seq'))
Inputs may be any that keep to these rules, and one draw needn't show every extreme that they name: `send_order`: each row names every local row once. `segment_ids`: ids never fall along a row; each document holds 1 to 512 tokens and one holds exactly that many. `w_query`: entries lie within -12 and 12 divided by the square root of 4096. `w_key`: entries lie within -12 and 12 divided by the square root of 4096.
All inputs are finite; a program needn't handle non-finite values.
Results may differ from a plain program's by a relative error of at most 0.0085.
The roundings to bfloat16 on the way count: a program that leaves them out, or rounds other values in their place, can miss the bound.
Values may be sent and summed in bfloat16 or wider, within the bound.
A program may use at most 128 MiB of HBM per device.

v0:
```python
import jax
import jax.numpy as jnp
from jax import lax
from jax.sharding import PartitionSpec as P

H = 32
G = 4
HD = 128


def attend_block(query_blk, seg_blk, first_row, keys, values, seg_keys, scale):
    count = keys.shape[0]
    scores = jnp.einsum("qhd,kd->hqk", query_blk, keys, preferred_element_type=jnp.float32) * scale
    rows_at = first_row + jnp.arange(query_blk.shape[0], dtype=jnp.int32)
    cols_at = jnp.arange(count, dtype=jnp.int32)
    visible = (seg_blk[:, None] == seg_keys[None, :]) & (rows_at[:, None] >= cols_at[None, :])
    scores = jnp.where(visible[None, :, :], scores, -jnp.inf)
    top = jnp.max(scores, axis=2, keepdims=True)
    weights = jnp.exp(scores - top)
    probs = (weights / jnp.sum(weights, axis=2, keepdims=True)).astype(jnp.bfloat16)
    mixed = jnp.einsum("hqk,kd->qhd", probs, values, preferred_element_type=jnp.float32)
    return mixed.astype(jnp.bfloat16).reshape(query_blk.shape[0], -1)


def per_device(tokens, norm_gain, send_order, segment_ids, w_query, w_key, w_value, w_out):
    seq_rank = lax.axis_index("seq")
    wide = tokens.astype(jnp.float32)
    square = jnp.mean(wide * wide, axis=1, keepdims=True)
    normed = (wide * lax.rsqrt(square + 1e-05) * norm_gain[None, :]).astype(jnp.bfloat16)
    sending = jnp.take(normed, send_order[0], axis=0)
    arrived = lax.all_to_all(sending, "dp", split_axis=0, concat_axis=0, tiled=True)
    heads_local = w_query.shape[1] // HD
    per_kv = H // G
    kv_index = seq_rank * heads_local // per_kv
    key_cols = lax.dynamic_slice_in_dim(w_key, kv_index * HD, HD, 1)
    value_cols = lax.dynamic_slice_in_dim(w_value, kv_index * HD, HD, 1)
    full_query, full_key, full_value, full_out = (
        lax.all_gather(w_query, "dp", axis=0, tiled=True),
        lax.all_gather(key_cols, "dp", axis=0, tiled=True),
        lax.all_gather(value_cols, "dp", axis=0, tiled=True),
        lax.all_gather(w_out, "dp", axis=1, tiled=True),
    )
    projection = jnp.concatenate([full_query, full_key, full_value], axis=1)
    qkv = jnp.dot(
        lax.all_gather(arrived, "seq", axis=0, tiled=True),
        projection,
        preferred_element_type=jnp.float32,
    ).astype(jnp.bfloat16)
    group_rows = qkv.shape[0]
    width_q = heads_local * HD
    query = qkv[:, :width_q].reshape(group_rows, heads_local, HD)
    keys = qkv[:, width_q : width_q + HD]
    values = qkv[:, width_q + HD :]
    seg = segment_ids[0]
    scale = HD ** (-0.5)
    block = min(512, group_rows)
    blocks = group_rows // block
    query_blocks = query.reshape(blocks, block, heads_local, HD)
    seg_blocks = seg.reshape(blocks, block)
    starts = jnp.arange(blocks, dtype=jnp.int32) * block

    def one_block(inputs):
        query_blk, seg_blk, first_row = inputs
        return attend_block(query_blk, seg_blk, first_row, keys, values, seg, scale)

    heads_out = lax.map(one_block, (query_blocks, seg_blocks, starts)).reshape(group_rows, width_q)
    result = lax.psum_scatter(
        jnp.dot(heads_out, full_out, preferred_element_type=jnp.float32),
        "seq",
        scatter_dimension=0,
        tiled=True,
    )
    leaving = lax.all_to_all(
        result.astype(jnp.bfloat16), "dp", split_axis=0, concat_axis=0, tiled=True
    )
    return jnp.zeros_like(leaving).at[send_order[0]].set(leaving)


def solution(mesh):
    return jax.shard_map(
        per_device,
        mesh=mesh,
        in_specs=(
            P(("dp", "seq"), None),
            P(),
            P(("dp", "seq"), None),
            P("dp", None),
            P("dp", "seq"),
            P("dp", None),
            P("dp", None),
            P("seq", "dp"),
        ),
        out_specs=P(("dp", "seq"), None),
        check_vma=False,
    )
```

profile of v0, /device:TPU:1, one launch (start us, length us, event | category | flops | bytes accessed | tf_op | source)
XLA Modules:
  0.0 405.3 jit_solution(5130573035376837800)
XLA Ops:
  6.5 0.9 copy-done
  7.5 0.6 constant_dynamic-slice_fusion.3
  8.2 1.5 constant_dynamic-slice_fusion.2
  9.7 0.7 all-gather.8.cloned.1.call-update
  10.5 0.5 broadcast.107
  11.0 1.2 reduce.7
  12.2 0.1 squeeze.17
  12.3 0.7 fusion.36
  13.0 1.5 fusion.27
  14.5 1.6 fusion.29
  16.1 1.2 gather_fusion
  17.3 0.2 bitcast_select_fusion
  17.5 24.3 %all_to_all.21 = bf16[16,8,4096]{2,1,0:T(8,128)(2,1)} all-to-all(bf16[16,8,4096]{2,1,0:T(8,128)(2,1)S(1)} %bitcast_select_fusion), channel_id=1, replica_groups=mesh['dp'=16,'seq'=8] {'dp'}, dimensions={0} | all-to-all | bytes 2097152 | tf_op jit(solution)/shard_map/all_to_all | solution.py:31
  41.8 0.5 all-gather.14.cloned.1.call-update
  42.4 0.6 reduce.6
  43.0 17.1 %all-gather.10.cloned.1.call-done = bf16[4096,128]{1,0:T(8,128)(2,1)} async-done(((bf16[256,128]{1,0:T(8,128)(2,1)}), bf16[4096,128]{1,0:T(8,128)(2,1)}) %all-gather.10.cloned.1.call-update) | async-done | bytes 1048592 | tf_op jit(solution)/shard_map/all_gather | solution.py:39
  60.1 44.0 %all-gather.12.cloned.1.call-done = bf16[4096,128]{1,0:T(8,128)(2,1)} async-done(((bf16[256,128]{1,0:T(8,128)(2,1)}), bf16[4096,128]{1,0:T(8,128)(2,1)}) %all-gather.12.cloned.1.call-update) | async-done | bytes 1048592 | tf_op jit(solution)/shard_map/all_gather | solution.py:40
  104.2 54.3 %all-gather.8.cloned.1.call-done = bf16[4096,512]{1,0:T(8,128)(2,1)} async-done(((bf16[256,512]{1,0:T(8,128)(2,1)}), bf16[4096,512]{1,0:T(8,128)(2,1)}) %all-gather.8.cloned.1.call-update) | async-done | bytes 4194320 | tf_op jit(solution)/shard_map/all_gather | solution.py:38
  158.4 51.7 %all-gather.6.cloned.1.call-done = bf16[1024,4096]{1,0:T(8,128)(2,1)} async-done(((bf16[128,4096]{1,0:T(8,128)(2,1)}), bf16[1024,4096]{1,0:T(8,128)(2,1)}) %all-gather.6.cloned.1.call-update) | async-done | bytes 8388624 | tf_op jit(solution)/shard_map/all_gather | solution.py:45
  210.1 11.8 %fusion.30 = bf16[1024,768]{1,0:T(8,128)(2,1)S(1)} fusion(bf16[1024,4096]{1,0:T(8,128)(2,1)} %all-gather.6.cloned.1.call-done, bf16[4096,128]{1,0:T(8,128)(2,1)} %all-gather.12.cloned.1.call-done, bf16[4096,128]{1,0:T(8,128)(2,1)} %all-gather.10.cloned.1.call-done, bf16[4096,512]{1,0:T(8,128)(2,1)} %all-gather.8.cloned.1.call-done), kind=kOutput, calls=%fused_computation.39 | convolution fusion | flops 6462111744 | bytes 16252928 | tf_op jit(solution)/shard_map/dot_general | solution.py:44
  222.0 1.2 copy-done.1
  223.1 0.1 slice.14
  223.2 0.5 reshape_reshape.3
  223.7 1.1 fusion.43
  224.8 0.1 copy.12
  224.9 26.7 %while.10 = (s32[]{:T(128)}, bf16[2,512,512]{2,1,0:T(8,128)(2,1)}, s32[2,512]{1,0:T(2,128)S(1)}, s32[1,1024]{1,0:T(1,128)S(1)}, s32[2]{0:T(128)S(1)}, /*index=5*...) while((s32[]{:T(128)}, bf16[2,512,512]{2,1,0:T(8,128)(2,1)}, ...), condition=%wide.region_4.5_spmd, body=%wide.region_1.4_spmd.sunk | while | flops 1088161280 | bytes 22575232 | solution.py:66
  224.9 0.6 dynamic_slice.29
  225.5 0.6 iota_add_fusion.2
  226.1 0.6 fusion.55
  226.7 0.2 constant_dynamic-slice_fusion.7
  226.9 5.3 %fusion.56 = (f32[4,512]{1,0:T(4,128)S(1)}, f32[4,512,1024]{2,1,0:T(8,128)}) fusion(pred[512,1024]{1,0:T(8,128)(4,1)S(1)} %fusion.55, bf16[1,512,4,128]{3,2,1,0:T(4,128)(2,1)S(1)} %constant_dynamic-slice_fusion.7, bf16[1024,128]{1,0:T(8,128)(2,1)S(1)} %get-tuple-element.161), kind=kOutput, calls=%fused_computation.55.clone.1 | convolution fusion | flops 545260544 | bytes 9707520 | tf_op jit(solution)/shard_map/while/body/eval_jaxpr/sub | solution.py:19
  232.2 5.0 %fusion.57 = bf16[4,512,128]{1,2,0:T(8,128)(2,1)S(1)} fusion(f32[4,512,1024]{2,1,0:T(8,128)} %get-tuple-element.135, f32[4,512]{1,0:T(4,128)S(1)} %get-tuple-element.136, bf16[1024,128]{0,1:T(8,128)(2,1)S(1)} %get-tuple-element.162), kind=kOutput, calls=%fused_computation.15.clone.1 | convolution fusion | flops 541327360 | bytes 9183232 | tf_op jit(solution)/shard_map/while/body/eval_jaxpr/hqk,kd->qhd/dot_general | solution.py:21
  237.2 0.2 copy.31
  237.4 0.8 constant_dynamic-update-slice_fusion.2
  238.3 0.6 dynamic_slice.29
  238.8 0.6 iota_add_fusion.2
  239.4 0.6 fusion.55
  240.0 0.2 constant_dynamic-slice_fusion.7
  240.2 5.3 %fusion.56 = (f32[4,512]{1,0:T(4,128)S(1)}, f32[4,512,1024]{2,1,0:T(8,128)}) fusion(pred[512,1024]{1,0:T(8,128)(4,1)S(1)} %fusion.55, bf16[1,512,4,128]{3,2,1,0:T(4,128)(2,1)S(1)} %constant_dynamic-slice_fusion.7, bf16[1024,128]{1,0:T(8,128)(2,1)S(1)} %get-tuple-element.161), kind=kOutput, calls=%fused_computation.55.clone.1 | convolution fusion | flops 545260544 | bytes 9707520 | tf_op jit(solution)/shard_map/while/body/eval_jaxpr/sub | solution.py:19
  245.5 5.0 %fusion.57 = bf16[4,512,128]{1,2,0:T(8,128)(2,1)S(1)} fusion(f32[4,512,1024]{2,1,0:T(8,128)} %get-tuple-element.135, f32[4,512]{1,0:T(4,128)S(1)} %get-tuple-element.136, bf16[1024,128]{0,1:T(8,128)(2,1)S(1)} %get-tuple-element.162), kind=kOutput, calls=%fused_computation.15.clone.1 | convolution fusion | flops 541327360 | bytes 9183232 | tf_op jit(solution)/shard_map/while/body/eval_jaxpr/hqk,kd->qhd/dot_general | solution.py:21
  250.5 0.2 copy.31
  250.8 0.8 constant_dynamic-update-slice_fusion.2
  251.6 16.7 %all-gather.14.cloned.1.call-done = bf16[512,4096]{1,0:T(8,128)(2,1)} async-done(((bf16[512,256]{1,0:T(8,128)(2,1)}), bf16[512,4096]{1,0:T(8,128)(2,1)}) %all-gather.14.cloned.1.call-update) | async-done | bytes 4194320 | tf_op jit(solution)/shard_map/all_gather | solution.py:41
  268.3 12.7 %fusion.44 = f32[1024,4096]{1,0:T(8,128)} fusion(bf16[1024,512]{1,0:T(8,128)(2,1)} %bitcast.80, bf16[512,4096]{1,0:T(8,128)(2,1)} %all-gather.14.cloned.1.call-done), kind=kOutput, calls=%fused_computation.57 | convolution fusion | flops 4294967296 | bytes 22020096 | tf_op jit(solution)/shard_map/dot_general | solution.py:68
  281.1 91.7 %reduce-scatter.2.cloned.1.call-done = f32[128,4096]{1,0:T(8,128)} async-done(((f32[1024,4096]{1,0:T(8,128)}), f32[128,4096]{1,0:T(8,128)}) %reduce-scatter.2.cloned.1.call-update) | async-done | bytes 2097168 | tf_op jit(solution)/shard_map/reduce_scatter | solution.py:67
  372.7 1.7 convert_bitcast_fusion
  374.5 20.9 %all_to_all.22 = bf16[16,8,4096]{2,1,0:T(8,128)(2,1)S(1)} all-to-all(bf16[16,8,4096]{2,1,0:T(8,128)(2,1)S(1)} %convert_bitcast_fusion), channel_id=1, replica_groups=mesh['dp'=16,'seq'=8] {'dp'}, dimensions={0} | all-to-all | bytes 2097152 | tf_op jit(solution)/shard_map/all_to_all | solution.py:73
  395.4 3.0 scatter_custom_fusion
  (22 shorter events, 0.3 us)
Async XLA Ops:
  6.5 1.0 copy-start
  6.5 53.6 %all-gather.10.cloned.1.call-start = ((), (), s32[]{:S(2)}) async-start(), calls=%async_computation.5 | async-start | bytes 1114112 | tf_op jit(solution)/shard_map/all_gather | solution.py:39
  8.1 96.0 %all-gather.12.cloned.1.call-start = ((), (), s32[]{:S(2)}) async-start(), calls=%async_computation.6 | async-start | bytes 1114112 | tf_op jit(solution)/shard_map/all_gather | solution.py:40
  9.7 148.8 %all-gather.8.cloned.1.call-start = ((), (), s32[]{:S(2)}) async-start(), calls=%async_computation.4 | async-start | bytes 4456448 | tf_op jit(solution)/shard_map/all_gather | solution.py:38
  10.4 199.7 %all-gather.6.cloned.1.call-start = ((), (), s32[]{:S(2)}) async-start(), calls=%async_computation.3 | async-start | bytes 9437184 | tf_op jit(solution)/shard_map/all_gather | solution.py:45
  16.1 26.4 %copy-start.2 = (s32[1,1024]{1,0:T(1,128)S(1)}, s32[1,1024]{1,0:T(1,128)}, u32[]{:S(2)}) copy-start(s32[1,1024]{1,0:T(1,128)} %param.13) | copy-start | bytes 12292
  41.8 226.5 %all-gather.14.cloned.1.call-start = ((), (), s32[]{:S(2)}) async-start(), calls=%async_computation.7 | async-start | bytes 4456448 | tf_op jit(solution)/shard_map/all_gather | solution.py:41
  42.4 330.4 %reduce-scatter.2.cloned.1.call-start = ((), (), s32[]{:S(2)}) async-start(), calls=%async_computation.8 | async-start | bytes 18874368 | tf_op jit(solution)/shard_map/reduce_scatter | solution.py:67
  222.0 1.2 copy-start.1
Sparse Core Ops, SparseCore 0:
  9.5 50.5 all-gather.9
  62.3 41.8 all-gather.11
  106.3 52.0 all-gather.7
  160.0 50.0 all-gather.5
  212.1 56.1 all-gather.13
  281.2 91.5 reduce-scatter.1
where the time goes:
time: 408 us; the launch traced here: 405 us
  waiting for transfers between devices  277 us (68%)
  blocking collectives  45.2 us (11%)
  matrix products  45.2 us (11%)
  local copies, waits for them, and re-layouts  14.5 us (4%)
  between operations  13.6 us (3%)
  other arithmetic  9.72 us (2%)
    reduce_scatter x1, waiting for transfers between devices, per_device(): lax.psum_scatter(jnp.dot(heads_out, full_out, preferred_element_type=jnp....  91.7 us
    all_gather x1, waiting for transfers between devices, per_device(): lax.all_gather(w_query, 'dp', axis=0, tiled=True)  54.3 us
    all_gather x1, waiting for transfers between devices, per_device(): lax.all_gather(arrived, 'seq', axis=0, tiled=True)  51.7 us
    all_gather x1, waiting for transfers between devices, per_device(): lax.all_gather(value_cols, 'dp', axis=0, tiled=True)  44 us
    all_to_all x1, blocking collectives, per_device(): lax.all_to_all(sending, 'dp', split_axis=0, concat_axis=0, tiled=True)  24.3 us
    all_to_all x1, blocking collectives, per_device(): lax.all_to_all(result.astype(jnp.bfloat16), 'dp', split_axis=0, concat_ax...  20.9 us
    all_gather x1, waiting for transfers between devices, per_device(): lax.all_gather(key_cols, 'dp', axis=0, tiled=True)  17.1 us
    all_gather x1, waiting for transfers between devices, per_device(): lax.all_gather(w_out, 'dp', axis=1, tiled=True)  16.7 us
  transfers between devices with their start and end apart: 6, of which 6 were waited for; matrix products, arithmetic and copies ran while one was open for 12% of the time, Pallas kernels for 0%

commit v1 on v0

v1 whole, which is shorter than its diff:
```python
import jax
import jax.numpy as jnp
from jax import lax
from jax.experimental import pallas as pl
from jax.experimental.pallas import tpu as pltpu
from jax.sharding import PartitionSpec as P

BF = jnp.bfloat16
F32 = jnp.float32
MESH = pl.DeviceIdType.MESH
NEG = float("-inf")
EXP_SCALE = 128 ** (-0.5) * 1.4426950408889634

M_SIB_ROWS = 0
M_SIB_WO = 1
M_SIB_KV = 2
M_SIB_X = 3
M_SIB_HO = 7
M_A2A = 11
M_Z = 27
M_W = 39
M_WO = 71
M_OPP = 103
M_FIN = 107
M_HOME = 115
M_COUNT = 147


class Gather:
    def __init__(self, base, view, rows, at, message):
        self.base, self.view, self.rows, self.at, self.message = base, view, rows, at, message

    def part(self, h, d1, d2, quarter=None):
        half = self.rows // 2
        if quarter is None:
            return self.view(self.at(h, d1, d2), h * half, half)
        return self.view(self.at(h, d1, d2), h * half + quarter * (half // 2), half // 2)

    def send(self, h, m, ref, d1, d2):
        self.message(self.base + 16 * h + m, ref, ref, (self.at(h, d1, d2), None)).start()

    def recv(self, h, m, ref):
        self.message(self.base + 16 * h + m, ref, ref, None).wait_recv()

    def own(self):
        for h in range(2):
            mine = self.part(h, 0, 0)
            self.send(h, 0, mine, 1, 0)
            self.send(h, 1, mine, -1, 0)
            self.send(h, 4, mine, 0, 1)
            self.send(h, 8, mine, 0, -1)

    def first(self):
        for h in range(2):
            ref = self.part(h, -1, 0)
            self.recv(h, 0, ref)
            self.send(h, 2, self.part(h, -1, 0, 0), 1, 0)
            self.send(h, 5, ref, 0, 1)
            self.send(h, 9, ref, 0, -1)
        for h in range(2):
            ref = self.part(h, 1, 0)
            self.recv(h, 1, ref)
            self.send(h, 3, self.part(h, 1, 0, 1), -1, 0)
            self.send(h, 6, ref, 0, 1)
            self.send(h, 10, ref, 0, -1)
        for h in range(2):
            ref = self.part(h, 0, -1)
            self.recv(h, 4, ref)
            self.send(h, 12, ref, 0, 1)
            self.recv(h, 8, self.part(h, 0, 1))

    def second(self):
        for h in range(2):
            self.recv(h, 2, self.part(h, 2, 0, 0))
            self.recv(h, 3, self.part(h, 2, 0, 1))
            ref = self.part(h, 2, 0)
            self.send(h, 7, ref, 0, 1)
            self.send(h, 11, ref, 0, -1)

    def third(self):
        for h in range(2):
            ref = self.part(h, -1, -1)
            self.recv(h, 5, ref)
            self.send(h, 13, ref, 0, 1)
            ref = self.part(h, 1, 1)
            self.recv(h, 10, ref)
            self.send(h, 14, ref, 0, -1)
        for h in range(2):
            self.recv(h, 9, self.part(h, -1, 1))
            self.recv(h, 6, self.part(h, 1, -1))
            ref = self.part(h, 2, 1)
            self.recv(h, 11, ref)
            self.send(h, 15, ref, 0, -1)
            self.recv(h, 7, self.part(h, 2, -1))

    def last(self):
        for h in range(2):
            self.recv(h, 12, self.part(h, 0, 2))
            self.recv(h, 13, self.part(h, -1, 2))
            self.recv(h, 14, self.part(h, 1, 2))
            self.recv(h, 15, self.part(h, 2, 2))

    def drain(self):
        for h in range(2):
            for m in range(16):
                ref = self.part(h, 0, 0, 0 if m in (2, 3) else None)
                self.message(self.base + 16 * h + m, ref, ref, None).wait_send()


def kernel(
    tok, gain, order, seg, wq, wk, wv, wo, out,
    x_buf, nb, sib, s_buf, wall, wob, qkv, ho, bias, p32, snd, opr, fin, fs, r_buf, pick,
    lsem, ssem, rsem,
):
    dp = lax.axis_index("dp")
    sq = lax.axis_index("seq")
    x, y = lax.div(dp, 4), lax.rem(dp, 4)
    z, c = lax.div(sq, 2), lax.rem(sq, 2)
    other = 1 - c

    def ring(v):
        return {0: v, 1: lax.rem(v + 1, 4), 2: lax.rem(v + 2, 4), -1: lax.rem(v + 3, 4), 3: lax.rem(v + 3, 4)}

    xr, yr, zr = ring(x), ring(y), ring(z)

    def plane(kx, ky):
        return xr[kx] * 4 + yr[ky]

    def message(index, src, dst, dev):
        if dev is None:
            dev = (dp, z * 2 + other)
        elif dev[1] is None:
            dev = (dev[0], sq)
        return pltpu.make_async_remote_copy(
            src_ref=src, dst_ref=dst, send_sem=ssem.at[index], recv_sem=rsem.at[index],
            device_id=dev, device_id_type=MESH,
        )

    sibling = (dp, z * 2 + other)
    z_up, z_down = (dp, zr[1] * 2 + c), (dp, zr[-1] * 2 + c)

    barrier = pltpu.get_barrier_semaphore()
    greeted = [sibling, z_up, z_down]
    for kx in range(4):
        for ky in range(4):
            if kx or ky:
                greeted.append((plane(kx, ky), sq))
                greeted.append((plane(kx, ky), z * 2 + other))
    for dev in greeted:
        pl.semaphore_signal(barrier, inc=1, device_id=dev, device_id_type=MESH)

    load_q = pltpu.make_async_copy(wq, wall.at[dp, :, pl.ds(128, 512)], lsem.at[0])
    load_q.start()
    load_o = pltpu.make_async_copy(
        wo.at[:, pl.ds(pl.multiple_of(c * 128, 128), 128)],
        wob.at[dp, pl.ds(pl.multiple_of(c * 512, 512), 512), :], lsem.at[2])
    load_o.start()
    kv_cols = pl.ds(pl.multiple_of(z * 128, 128), 128)

    @pl.when(c == 0)
    def _():
        load = pltpu.make_async_copy(wk.at[:, kv_cols], wall.at[dp, :, pl.ds(0, 128)], lsem.at[1])
        load.start()
        load.wait()

    @pl.when(c == 1)
    def _():
        load = pltpu.make_async_copy(wv.at[:, kv_cols], wall.at[dp, :, pl.ds(640, 128)], lsem.at[1])
        load.start()
        load.wait()

    load_q.wait()
    pl.semaphore_wait(barrier, len(greeted))

    def at(h, d1, d2):
        return xr[d2] * 4 + yr[d1] if h == 0 else xr[d1] * 4 + yr[d2]

    own_cols = pl.ds(pl.multiple_of(c * 128, 128), 640)
    gather_w = Gather(M_W, lambda j, lo, n: wall.at[j, pl.ds(lo, n), own_cols], 256, at, message)
    gather_o = Gather(M_WO, lambda j, lo, n: wob.at[j, pl.ds(lo, n), :], 1024, at, message)
    gather_w.own()
    wo_slot = wob.at[dp, pl.ds(pl.multiple_of(c * 512, 512), 512), :]
    sib_wo = message(M_SIB_WO, wo.at[:, pl.ds(pl.multiple_of(other * 128, 128), 128)], wo_slot, sibling)
    sib_wo.start()

    def norm_rows(i, carry):
        rows = pl.ds(pl.multiple_of(i * 16, 16), 16)
        wide = tok[rows, :].astype(F32)
        square = jnp.mean(wide * wide, axis=1, keepdims=True)
        normed = (wide * lax.rsqrt(square + 1e-05) * gain[...]).astype(BF)
        out[rows, :] = normed
        return carry

    lax.fori_loop(0, 8, norm_rows, 0)

    to_home = (order[...] == lax.broadcasted_iota(jnp.int32, (128, 128), 0)).astype(F32)
    to_send = to_home.T.astype(BF)

    def permute(i, carry):
        cols = pl.ds(pl.multiple_of(i * 512, 512), 512)
        for h in range(2):
            src = pl.ds(pl.multiple_of(h * 2048 + i * 512, 512), 512)
            nb[h, :, cols] = jnp.dot(to_send, out[:, src], preferred_element_type=F32).astype(BF)
        return carry

    lax.fori_loop(0, 4, permute, 0)
    sib_rows = message(M_SIB_ROWS, nb.at[other], sib, sibling)
    sib_rows.start()

    column = lax.broadcasted_iota(jnp.int32, (128, 256), 1)
    source = lax.div(column, 16) * 8 + lax.rem(column, 8)
    for h in range(2):
        spread = (lax.broadcasted_iota(jnp.int32, (128, 256), 0) == source) & (lax.rem(lax.div(column, 8), 2) == h)
        pick[h] = jnp.dot(to_home.astype(BF), spread.astype(F32).astype(BF), preferred_element_type=F32).astype(BF)

    sib_rows.wait_recv()

    def interleave(i, carry):
        cols = pl.ds(pl.multiple_of(i * 256, 256), 256)
        mine = nb[c, :, cols].astype(F32)
        his = sib[:, cols].astype(F32)
        low = jnp.where(c == 0, mine, his).reshape(16, 1, 8, 256)
        high = jnp.where(c == 0, his, mine).reshape(16, 1, 8, 256)
        s_buf[:, cols] = jnp.concatenate([low, high], axis=1).reshape(256, 256).astype(BF)
        return carry

    lax.fori_loop(0, 8, interleave, 0)

    def x_rows(half, zz, row, count):
        return x_buf.at[half, pl.ds(pl.multiple_of(zz * 256 + row, 16), count), :]

    def piece(j):
        return s_buf.at[pl.ds(pl.multiple_of(j * 16, 16), 16), :]

    for kx in range(4):
        for ky in range(4):
            if kx or ky:
                j = plane(kx, ky)
                message(M_A2A + kx * 4 + ky, piece(j), x_rows(c, z, dp * 16, 16), (j, sq)).start()
    x_buf[c, pl.ds(pl.multiple_of(z * 256 + dp * 16, 16), 16), :] = s_buf[pl.ds(pl.multiple_of(dp * 16, 16), 16), :]

    def mask_rows(qb, carry):
        seg_q = seg[:, pl.ds(pl.multiple_of(qb * 128, 128), 128)].astype(F32)
        seg_q = jnp.broadcast_to(seg_q, (128, 128)).T
        start = jnp.maximum(qb - 4, 0) * 128
        row_at = qb * 128 + lax.broadcasted_iota(jnp.int32, (128, 128), 0)
        for k in range(5):
            seg_k = seg[:, pl.ds(pl.multiple_of(start + k * 128, 128), 128)].astype(F32)
            col_at = start + k * 128 + lax.broadcasted_iota(jnp.int32, (128, 128), 1)
            visible = (seg_q == seg_k) & (row_at >= col_at)
            bias[qb, :, k * 128 : (k + 1) * 128] = jnp.where(visible, 0.0, NEG)
        return carry

    gather_w.first()
    lax.fori_loop(0, 8, mask_rows, 0)

    def to_sibling(rel, row):
        ref = x_rows(c, zr[rel], row, 64)
        message(M_SIB_X + (rel % 4), ref, ref, sibling).start()

    def arrived(kx):
        for ky in range(4):
            if kx or ky:
                j = plane(-kx if kx == 1 else (1 if kx == 3 else kx), -ky if ky == 1 else (1 if ky == 3 else ky))
                ref = x_rows(c, z, j * 16, 16)
                message(M_A2A + kx * 4 + ky, ref, ref, None).wait_recv()
        row = xr[(4 - kx) % 4] * 64
        ref = x_rows(c, z, row, 64)
        message(M_Z + kx, ref, ref, z_up).start()
        message(M_Z + 4 + kx, ref, ref, z_down).start()
        to_sibling(0, row)

    def passed(kx):
        row = xr[(4 - kx) % 4] * 64
        low = x_rows(c, zr[-1], row, 64)
        message(M_Z + kx, low, low, None).wait_recv()
        if kx % 2 == 0:
            message(M_Z + 8 + kx, low, low, z_up).start()
        to_sibling(-1, row)
        high = x_rows(c, zr[1], row, 64)
        message(M_Z + 4 + kx, high, high, None).wait_recv()
        if kx % 2 == 1:
            message(M_Z + 8 + kx, high, high, z_down).start()
        to_sibling(1, row)

    def opposite(kx):
        row = xr[(4 - kx) % 4] * 64
        ref = x_rows(c, zr[2], row, 64)
        message(M_Z + 8 + kx, ref, ref, None).wait_recv()
        to_sibling(2, row)

    arrived(0)
    arrived(1)
    arrived(2)
    arrived(3)
    gather_w.second()
    passed(0)
    gather_w.third()
    passed(1)
    load_o.wait()
    sib_slot = wob.at[dp, pl.ds(pl.multiple_of(other * 512, 512), 512), :]
    message(M_SIB_WO, sib_slot, sib_slot, None).wait_recv()
    gather_w.last()
    kv_sent = wall.at[:, :, pl.ds(pl.multiple_of(c * 640, 128), 128)]
    kv_came = wall.at[:, :, pl.ds(pl.multiple_of(other * 640, 128), 128)]
    message(M_SIB_KV, kv_sent, kv_sent, sibling).start()
    gather_o.own()
    passed(2)
    passed(3)
    message(M_SIB_KV, kv_came, kv_came, None).wait_recv()

    def project(rel):
        zz = zr[rel]
        ref = x_rows(other, zz, 0, 256)
        message(M_SIB_X + (rel % 4), ref, ref, None).wait_recv()
        rows = pl.ds(pl.multiple_of(zz * 256, 256), 256)

        def columns(n, carry):
            cols = pl.ds(pl.multiple_of(n * 256, 256), 256)
            acc = jnp.dot(x_buf[0, rows, :], wall[0:8, :, cols].reshape(2048, 256), preferred_element_type=F32)
            acc += jnp.dot(x_buf[1, rows, :], wall[8:16, :, cols].reshape(2048, 256), preferred_element_type=F32)
            acc = jnp.transpose(acc.reshape(16, 2, 8, 256), (1, 0, 2, 3)).reshape(256, 256)
            qkv[rows, cols] = acc.astype(BF)
            return carry

        lax.fori_loop(0, 3, columns, 0)

    project(0)
    gather_o.first()
    project(-1)
    gather_o.second()
    project(1)
    for kx in range(4):
        opposite(kx)
    gather_o.third()
    project(2)
    gather_o.last()

    def block(i, carry):
        zz = lax.rem(z + 2 - i + 3 * lax.div(i, 2) - 2 * lax.div(i, 3) + 4, 4)

        def attend(half, carry):
            qb = zz * 2 + half
            rows = pl.ds(pl.multiple_of(qb * 128, 128), 128)
            window = pl.ds(pl.multiple_of(jnp.maximum(qb - 4, 0) * 128, 128), 640)
            query = jnp.concatenate([qkv[rows, 128 + 128 * h : 256 + 128 * h] for h in range(4)], axis=0)
            keys, values = qkv[window, 0:128], qkv[window, 640:768]
            scores = lax.dot_general(query, keys, (((1,), (1,)), ((), ())), preferred_element_type=F32)
            scores = scores.reshape(4, 128, 640) + bias[qb][None]
            top = jnp.max(scores, axis=2, keepdims=True)
            weights = jnp.exp2((scores - top) * EXP_SCALE)
            total = jnp.sum(weights, axis=2, keepdims=True).reshape(512, 1)
            mixed = jnp.dot(weights.astype(BF).reshape(512, 640), values, preferred_element_type=F32) / total
            for h in range(4):
                ho[c, rows, 128 * h : 128 * h + 128] = mixed[128 * h : 128 * h + 128].astype(BF)
            return carry

        lax.fori_loop(0, 2, attend, 0)
        rows = pl.ds(pl.multiple_of(zz * 256, 256), 256)
        message(M_SIB_HO + i, ho.at[c, rows, :], ho.at[c, rows, :], sibling).start()
        message(M_SIB_HO + i, ho.at[other, rows, :], ho.at[other, rows, :], None).wait_recv()

        def columns(n, carry):
            cols = pl.ds(pl.multiple_of(n * 256, 256), 256)
            lhs = jnp.concatenate([ho[0, rows, :], ho[1, rows, :]], axis=1)
            rhs = jnp.concatenate([wob[2 * n], wob[2 * n + 1]], axis=1)
            acc = jnp.dot(lhs, rhs, preferred_element_type=F32)
            acc = jnp.transpose(acc.reshape(2, 16, 8, 256), (1, 0, 2, 3)).reshape(4, 64, 256)
            for xs in range(4):
                kx = lax.rem(xs - x + 4, 4)
                p32[i, kx, :, cols] = acc[xs]
                snd[i, kx, :, cols] = acc[xs].astype(BF)
            return carry

        lax.fori_loop(0, 8, columns, 0)

        @pl.when(i == 0)
        def _():
            for kx in (0, 2, 1, 3):
                message(M_OPP + kx, snd.at[0, kx], opr.at[kx], z_up if kx < 2 else z_down).start()

        @pl.when(i == 1)
        def _():
            for kx in (2, 3):
                message(M_FIN + kx, snd.at[1, kx], fin.at[0, kx], z_up).start()

        @pl.when(i == 2)
        def _():
            for kx in (0, 1):
                message(M_FIN + 4 + kx, snd.at[2, kx], fin.at[1, kx], z_down).start()

        return carry

    lax.fori_loop(0, 4, block, 0)

    for kx in (0, 2, 1, 3):
        side = 0 if kx < 2 else 1
        message(M_OPP + kx, opr.at[kx], opr.at[kx], None).wait_recv()
        snd[1 + side, kx] = (p32[1 + side, kx] + opr[kx].astype(F32)).astype(BF)
        message(M_FIN + 4 * side + kx, snd.at[1 + side, kx], fin.at[side, kx], z_down if side else z_up).start()

    for kx in (0, 2, 1, 3):
        for side in range(2):
            message(M_FIN + 4 * side + kx, fin.at[side, kx], fin.at[side, kx], None).wait_recv()
        for yy in range(4):
            for core in range(2):
                rows = slice(yy * 16 + core * 8, yy * 16 + core * 8 + 8)
                rows2 = slice(yy * 16, yy * 16 + 16)
                tot = p32[3, kx, rows, :]
                for side in range(2):
                    tot = tot + fin[side, kx, rows2, :].astype(F32)[core * 8 : core * 8 + 8]
                fs[kx, yy, core] = jnp.concatenate([tot[:, :1024], tot[:, 1024:]], axis=0).astype(BF)
        for ky in range(4):
            for kc in range(2):
                core = c if kc == 0 else other
                src, dst = fs.at[kx, yr[ky], core], r_buf.at[c, dp]
                if kx or ky or kc:
                    message(M_HOME + kx * 8 + ky * 2 + kc, src, dst, (plane(kx, ky), z * 2 + core)).start()
                else:
                    keep = pltpu.make_async_copy(src, dst, lsem.at[3])
                    keep.start()

    keep.wait()
    for kx in (0, 2, 1, 3):
        for ky in range(4):
            for kc in range(2):
                if kx or ky or kc:
                    j = xr[(4 - kx) % 4] * 4 + yr[(4 - ky) % 4]
                    ref = r_buf.at[c if kc == 0 else other, j]
                    message(M_HOME + kx * 8 + ky * 2 + kc, ref, ref, None).wait_recv()

    for core in range(2):
        for h in range(2):
            back = jnp.dot(pick[h], r_buf[core].reshape(256, 1024), preferred_element_type=F32).astype(BF)
            for i in range(8):
                at_col = (h * 8 + i) * 256 + core * 128
                out[:, at_col : at_col + 128] = back[:, i * 128 : i * 128 + 128]

    sib_rows.wait_send()
    sib_wo.wait_send()
    message(M_SIB_KV, kv_sent, kv_sent, None).wait_send()
    for rel in range(4):
        ref = x_rows(c, zr[rel], 0, 256)
        message(M_SIB_X + rel, ref, ref, None).wait_send()
        ref = ho.at[c, pl.ds(0, 256), :]
        message(M_SIB_HO + rel, ref, ref, None).wait_send()
    for k in range(1, 16):
        message(M_A2A + k, piece(dp), piece(dp), None).wait_send()
    for k in range(12):
        ref = x_rows(c, z, 0, 64)
        message(M_Z + k, ref, ref, None).wait_send()
    gather_w.drain()
    gather_o.drain()
    for kx in range(4):
        message(M_OPP + kx, snd.at[0, kx], opr.at[kx], None).wait_send()
        for side in range(2):
            message(M_FIN + 4 * side + kx, snd.at[1 + side, kx], fin.at[side, kx], None).wait_send()
    for k in range(1, 32):
        message(M_HOME + k, fs.at[0, 0, 0], r_buf.at[0, 0], None).wait_send()


def per_device(tokens, norm_gain, send_order, segment_ids, w_query, w_key, w_value, w_out):
    vmem = pl.BlockSpec(memory_space=pltpu.VMEM)
    hbm = pl.BlockSpec(memory_space=pl.ANY)
    return pl.pallas_call(
        kernel,
        out_shape=jax.ShapeDtypeStruct((128, 4096), BF),
        in_specs=[vmem] * 4 + [hbm] * 4,
        out_specs=vmem,
        scratch_shapes=[
            pltpu.VMEM((2, 1024, 2048), BF),
            pltpu.VMEM((2, 128, 2048), BF),
            pltpu.VMEM((128, 2048), BF),
            pltpu.VMEM((256, 2048), BF),
            pltpu.VMEM((16, 256, 768), BF),
            pltpu.VMEM((16, 1024, 128), BF),
            pltpu.VMEM((1024, 768), BF),
            pltpu.VMEM((2, 1024, 512), BF),
            pltpu.VMEM((8, 128, 640), F32),
            pltpu.VMEM((4, 4, 64, 2048), F32),
            pltpu.VMEM((4, 4, 64, 2048), BF),
            pltpu.VMEM((4, 64, 2048), BF),
            pltpu.VMEM((2, 4, 64, 2048), BF),
            pltpu.VMEM((4, 4, 2, 16, 1024), BF),
            pltpu.VMEM((2, 16, 16, 1024), BF),
            pltpu.VMEM((2, 128, 256), BF),
            pltpu.SemaphoreType.DMA((4,)),
            pltpu.SemaphoreType.DMA((M_COUNT,)),
            pltpu.SemaphoreType.DMA((M_COUNT,)),
        ],
        compiler_params=pltpu.CompilerParams(
            collective_id=0, has_side_effects=True, vmem_limit_bytes=60 * 1024 * 1024
        ),
    )(tokens, norm_gain.reshape(1, 4096), send_order, segment_ids, w_query, w_key, w_value, w_out)


def solution(mesh):
    return jax.shard_map(
        per_device,
        mesh=mesh,
        in_specs=(
            P(("dp", "seq"), None),
            P(),
            P(("dp", "seq"), None),
            P("dp", None),
            P("dp", "seq"),
            P("dp", None),
            P("dp", None),
            P("seq", "dp"),
        ),
        out_specs=P(("dp", "seq"), None),
        check_vma=False,
    )
```

time: 408 us -> 136 us (0.33)
  waiting for transfers between devices: 277 us -> 0 us
  Pallas kernels: 0 us -> 133 us
  matrix products: 45.2 us -> 0 us
  blocking collectives: 45.2 us -> 0 us
  between operations: 13.6 us -> 0.01 us
  local copies, waits for them, and re-layouts: 14.5 us -> 2.29 us
  other arithmetic: 9.72 us -> 0 us
    all_gather x5 -> x0, waiting for transfers between devices: 184 us -> none  [the longest x1 54.3 us: per_device(): lax.all_gather(w_query, 'dp', axis=0, tiled=True)]
    pallas_call x0 -> x1, Pallas kernels: none -> 133 us  [per_device(): pl.pallas_call(kernel, out_shape=jax.ShapeDtypeStruct((128, 4096), BF), i...]
    reduce_scatter x1 -> x0, waiting for transfers between devices: 91.7 us -> none  [per_device(): lax.psum_scatter(jnp.dot(heads_out, full_out, preferred_element_type=jnp....]
    all_to_all x2 -> x0, blocking collectives: 45.2 us -> none  [the longest x1 24.3 us: per_device(): lax.all_to_all(sending, 'dp', split_axis=0, concat_axis=0, tiled=True)]
    dot_general x4 -> x0, matrix products: 34.6 us -> none  [the longest x1 12.7 us: per_device(): jnp.dot(heads_out, full_out, preferred_element_type=jnp.float32)]
    sub x2 -> x0, matrix products: 10.6 us -> none  [attend_block(): weights = jnp.exp(scores - top)]
  transfers between devices with their start and end apart: 6 -> 0, of which waited for: 6 -> 0; matrix products, arithmetic and copies ran while one was open for 12% -> 0% of each run, Pallas kernels for 0% -> 0%
where the time goes in v1:
time: 136 us
  Pallas kernels  133 us (98%)
  local copies, waits for them, and re-layouts  2.29 us (2%)
    pallas_call x1, Pallas kernels, per_device(): pl.pallas_call(kernel, out_shape=jax.ShapeDtypeStruct((128, 4096), BF), i...  133 us

profile of v1, /device:TPU:1, one launch (start us, length us, event | category | flops | bytes accessed | tf_op | source)
XLA Modules:
  0.0 135.7 jit_solution(10958743696804736017)
XLA Ops:
  0.0 133.4 %shard_map.82 = bf16[128,4096]{1,0:T(8,128)(2,1)} custom-call(bf16[128,4096]{1,0:T(8,128)(2,1)} %tok.1, f32[1,4096]{1,0:T(1,128)} %bitcast.1, s32[1,128]{1,0:T(1,128)} %order.1, s32[1,1024]{1,0:T(1,128)} %seg.1, bf16[256,512]{1,0:T(8,128)(2,1)} %wq.1, bf16[256,512]{1,0:T(8,128)(2,1)} %wk.1, bf16[256,512]{1,0:T(8,128)(2,1)} %wv.1, bf16[512,256]{1,0:T(8,128)(2,1)} %wo.1), custom_call_target="tpu_custom_call" | custom-call | tf_op jit(solution)/shard_map/pallas_call | solution.py:465
  133.4 2.3 %copy.10 = bf16[128,4096]{1,0:T(8,128)(2,1)} copy(bf16[128,4096]{1,0:T(8,128)(2,1)} %shard_map.82) | data formatting | bytes 2097152

commit v2 on v1

v2 whole, which is shorter than its diff:
```python
import jax
import jax.numpy as jnp
from jax import lax
from jax.experimental import pallas as pl
from jax.experimental.pallas import tpu as pltpu
from jax.sharding import PartitionSpec as P

BF = jnp.bfloat16
F32 = jnp.float32
MESH = pl.DeviceIdType.MESH
NEG = float("-inf")
EXP_SCALE = 128 ** (-0.5) * 1.4426950408889634

M_SIB_ROWS = 0
M_SIB_WO = 1
M_SIB_KV = 2
M_SIB_X = 3
M_SIB_HO = 7
M_A2A = 11
M_Z = 27
M_W = 75
M_WO = 107
M_OPP = 139
M_FIN = 147
M_HOME = 163
M_COUNT = 195

OFFSETS = (
    (0, 0), (1, 0), (3, 0), (0, 1), (0, 3), (2, 0), (0, 2), (1, 1), (3, 3), (1, 3), (3, 1),
    (2, 1), (2, 3), (1, 2), (3, 2), (2, 2),
)


class Gather:
    PLACE = {
        0: (-1, 0), 1: (1, 0), 2: (2, 0), 3: (2, 0), 4: (0, -1), 5: (-1, -1), 6: (1, -1), 7: (2, -1),
        8: (0, 1), 9: (-1, 1), 10: (1, 1), 11: (2, 1), 12: (0, 2), 13: (-1, 2), 14: (1, 2), 15: (2, 2),
    }
    ONWARD = {
        0: ((2, 1, 0), (5, 0, 1), (9, 0, -1)), 1: ((3, -1, 0), (6, 0, 1), (10, 0, -1)),
        3: ((7, 0, 1), (11, 0, -1)), 4: ((12, 0, 1),), 5: ((13, 0, 1),), 10: ((14, 0, -1),), 11: ((15, 0, -1),),
    }

    def __init__(self, base, view, rows, at, message):
        self.base, self.view, self.rows, self.at, self.message = base, view, rows, at, message

    def part(self, h, d1, d2, quarter=None):
        half = self.rows // 2
        if quarter is None:
            return self.view(self.at(h, d1, d2), h * half, half)
        return self.view(self.at(h, d1, d2), h * half + quarter * (half // 2), half // 2)

    def send(self, h, m, ref, d1, d2):
        self.message(self.base + 16 * h + m, ref, ref, (self.at(h, d1, d2), None)).start()

    def own(self):
        for h in range(2):
            mine = self.part(h, 0, 0)
            self.send(h, 0, mine, 1, 0)
            self.send(h, 1, mine, -1, 0)
            self.send(h, 4, mine, 0, 1)
            self.send(h, 8, mine, 0, -1)

    def take(self, *messages, halves=(0, 1)):
        for m in messages:
            for h in halves:
                d1, d2 = self.PLACE[m]
                ref = self.part(h, d1, d2, m - 2 if m in (2, 3) else None)
                self.message(self.base + 16 * h + m, ref, ref, None).wait_recv()
                for then, s1, s2 in self.ONWARD.get(m, ()):
                    self.send(h, then, self.part(h, d1, d2, then - 2 if then in (2, 3) else None), s1, s2)

    def drain(self):
        for h in range(2):
            for m in range(16):
                ref = self.part(h, 0, 0, 0 if m in (2, 3) else None)
                self.message(self.base + 16 * h + m, ref, ref, None).wait_send()


def kernel(
    tok_hbm, gain, order, seg, wq, wk, wv, wo, out,
    tok, x_buf, nb, sib, s_buf, wall, wob, qkv, ho, bias, p32, snd, opr, fin, fs, r_buf, pick,
    lsem, ssem, rsem,
):
    dp = lax.axis_index("dp")
    sq = lax.axis_index("seq")
    x, y = lax.div(dp, 4), lax.rem(dp, 4)
    z, c = lax.div(sq, 2), lax.rem(sq, 2)
    other = 1 - c

    load_tok = [
        pltpu.make_async_copy(tok_hbm.at[pl.ds(64 * k, 64), :], tok.at[pl.ds(64 * k, 64), :], lsem.at[4 + k])
        for k in range(2)
    ]
    load_tok[0].start()
    load_tok[1].start()

    def ring(v):
        return {0: v, 1: lax.rem(v + 1, 4), 2: lax.rem(v + 2, 4), -1: lax.rem(v + 3, 4), 3: lax.rem(v + 3, 4)}

    xr, yr, zr = ring(x), ring(y), ring(z)

    def plane(kx, ky):
        return xr[kx] * 4 + yr[ky]

    def back(kx, ky):
        return xr[(4 - kx) % 4] * 4 + yr[(4 - ky) % 4]

    def message(index, src, dst, dev):
        if dev is None:
            dev = (dp, z * 2 + other)
        elif dev[1] is None:
            dev = (dev[0], sq)
        return pltpu.make_async_remote_copy(
            src_ref=src, dst_ref=dst, send_sem=ssem.at[index], recv_sem=rsem.at[index],
            device_id=dev, device_id_type=MESH,
        )

    sibling = (dp, z * 2 + other)
    z_up, z_down = (dp, zr[1] * 2 + c), (dp, zr[-1] * 2 + c)

    load_q = pltpu.make_async_copy(wq, wall.at[dp, :, pl.ds(128, 512)], lsem.at[0])
    load_q.start()
    load_o = pltpu.make_async_copy(
        wo.at[:, pl.ds(pl.multiple_of(c * 128, 128), 128)],
        wob.at[dp, pl.ds(pl.multiple_of(c * 512, 512), 512), :], lsem.at[2])
    load_o.start()
    kv_cols = pl.ds(pl.multiple_of(z * 128, 128), 128)
    load_k = pltpu.make_async_copy(wk.at[:, kv_cols], wall.at[dp, :, pl.ds(0, 128)], lsem.at[1])
    load_v = pltpu.make_async_copy(wv.at[:, kv_cols], wall.at[dp, :, pl.ds(640, 128)], lsem.at[1])

    @pl.when(c == 0)
    def _():
        load_k.start()

    @pl.when(c == 1)
    def _():
        load_v.start()

    barrier = pltpu.get_barrier_semaphore()
    greeted = [sibling, z_up, z_down]
    for kx in range(4):
        for ky in range(4):
            if kx or ky:
                greeted.append((plane(kx, ky), sq))
                greeted.append((plane(kx, ky), z * 2 + other))
    for dev in greeted:
        pl.semaphore_signal(barrier, inc=1, device_id=dev, device_id_type=MESH)

    def norm_rows(i, carry):
        rows = pl.ds(pl.multiple_of(i * 16, 16), 16)
        wide = tok[rows, :].astype(F32)
        square = jnp.mean(wide * wide, axis=1, keepdims=True)
        out[rows, :] = (wide * lax.rsqrt(square + 1e-05) * gain[...]).astype(BF)
        return carry

    load_tok[0].wait()
    lax.fori_loop(0, 4, norm_rows, 0)
    load_tok[1].wait()

    @pl.when(c == 0)
    def _():
        load_k.wait()

    @pl.when(c == 1)
    def _():
        load_v.wait()

    load_q.wait()
    pl.semaphore_wait(barrier, len(greeted))

    def at(h, d1, d2):
        return xr[d2] * 4 + yr[d1] if h == 0 else xr[d1] * 4 + yr[d2]

    own_cols = pl.ds(pl.multiple_of(c * 128, 128), 640)
    gather_w = Gather(M_W, lambda j, lo, n: wall.at[j, pl.ds(lo, n), own_cols], 256, at, message)
    gather_o = Gather(M_WO, lambda j, lo, n: wob.at[j, pl.ds(lo, n), :], 1024, at, message)
    gather_w.own()
    lax.fori_loop(4, 8, norm_rows, 0)

    to_home = (order[...] == lax.broadcasted_iota(jnp.int32, (128, 128), 0)).astype(F32)
    to_send = to_home.T.astype(BF)

    def permute(i, carry):
        cols = pl.ds(pl.multiple_of(i * 512, 512), 512)
        nb[carry, :, cols] = jnp.dot(
            to_send, out[:, pl.ds(pl.multiple_of(carry * 2048 + i * 512, 512), 512)], preferred_element_type=F32
        ).astype(BF)
        return carry

    lax.fori_loop(0, 4, permute, other)
    sib_rows = message(M_SIB_ROWS, nb.at[other], sib, sibling)
    sib_rows.start()
    lax.fori_loop(0, 4, permute, c)
    sib_rows.wait_recv()

    def interleave(i, carry):
        cols = pl.ds(pl.multiple_of(i * 256, 256), 256)
        mine = nb[c, :, cols].astype(F32)
        his = sib[:, cols].astype(F32)
        low = jnp.where(c == 0, mine, his).reshape(16, 1, 8, 256)
        high = jnp.where(c == 0, his, mine).reshape(16, 1, 8, 256)
        s_buf[:, cols] = jnp.concatenate([low, high], axis=1).reshape(256, 256).astype(BF)
        return carry

    lax.fori_loop(0, 8, interleave, 0)

    def x_rows(half, zz, row, count):
        return x_buf.at[half, pl.ds(pl.multiple_of(zz * 256 + row, 16), count), :]

    def piece(j):
        return s_buf.at[pl.ds(pl.multiple_of(j * 16, 16), 16), :]

    for kx, ky in OFFSETS[1:]:
        j = plane(kx, ky)
        message(M_A2A + kx * 4 + ky, piece(j), x_rows(c, z, dp * 16, 16), (j, sq)).start()
    x_buf[c, pl.ds(pl.multiple_of(z * 256 + dp * 16, 16), 16), :] = s_buf[pl.ds(pl.multiple_of(dp * 16, 16), 16), :]

    def to_sibling(rel, row):
        ref = x_rows(c, zr[rel], row, 16)
        message(M_SIB_X + (rel % 4), ref, ref, sibling).start()

    def arrived(e):
        kx, ky = OFFSETS[e]
        row = back(kx, ky) * 16
        ref = x_rows(c, z, row, 16)
        if kx or ky:
            message(M_A2A + kx * 4 + ky, ref, ref, None).wait_recv()
        message(M_Z + e, ref, ref, z_up).start()
        message(M_Z + 16 + e, ref, ref, z_down).start()
        to_sibling(0, row)

    def passed(e):
        row = back(*OFFSETS[e]) * 16
        low = x_rows(c, zr[-1], row, 16)
        message(M_Z + e, low, low, None).wait_recv()
        if e % 2 == 0:
            message(M_Z + 32 + e, low, low, z_up).start()
        to_sibling(-1, row)
        high = x_rows(c, zr[1], row, 16)
        message(M_Z + 16 + e, high, high, None).wait_recv()
        if e % 2 == 1:
            message(M_Z + 32 + e, high, high, z_down).start()
        to_sibling(1, row)

    def opposite(e):
        row = back(*OFFSETS[e]) * 16
        ref = x_rows(c, zr[2], row, 16)
        message(M_Z + 32 + e, ref, ref, None).wait_recv()
        to_sibling(2, row)

    arrived(0)
    wo_slot = wob.at[dp, pl.ds(pl.multiple_of(c * 512, 512), 512), :]
    sib_wo = message(M_SIB_WO, wo.at[:, pl.ds(pl.multiple_of(other * 128, 128), 128)], wo_slot, sibling)
    sib_wo.start()
    for e in range(1, 5):
        arrived(e)
    gather_w.take(0, 1)

    def mask_rows(qb, carry):
        seg_q = seg[:, pl.ds(pl.multiple_of(qb * 128, 128), 128)].astype(F32)
        seg_q = jnp.broadcast_to(seg_q, (128, 128)).T
        start = jnp.maximum(qb - 4, 0) * 128
        row_at = qb * 128 + lax.broadcasted_iota(jnp.int32, (128, 128), 0)
        for k in range(5):
            seg_k = seg[:, pl.ds(pl.multiple_of(start + k * 128, 128), 128)].astype(F32)
            col_at = start + k * 128 + lax.broadcasted_iota(jnp.int32, (128, 128), 1)
            visible = (seg_q == seg_k) & (row_at >= col_at)
            bias[qb, :, k * 128 : (k + 1) * 128] = jnp.where(visible, 0.0, NEG)
        return carry

    lax.fori_loop(0, 8, mask_rows, 0)
    for e in range(5, 11):
        arrived(e)
    gather_w.take(4, 8)
    for e in range(11, 16):
        arrived(e)

    column = lax.broadcasted_iota(jnp.int32, (128, 256), 1)
    source = lax.div(column, 16) * 8 + lax.rem(column, 8)
    for h in range(2):
        spread = (lax.broadcasted_iota(jnp.int32, (128, 256), 0) == source) & (lax.rem(lax.div(column, 8), 2) == h)
        pick[h] = jnp.dot(to_home.astype(BF), spread.astype(F32).astype(BF), preferred_element_type=F32).astype(BF)

    gather_w.take(2, 3, 5, 10)
    for e in range(0, 8):
        passed(e)
    gather_w.take(11, 9, 6, 7)
    load_o.wait()
    sib_slot = wob.at[dp, pl.ds(pl.multiple_of(other * 512, 512), 512), :]
    message(M_SIB_WO, sib_slot, sib_slot, None).wait_recv()
    gather_o.own()
    for e in range(8, 16):
        passed(e)
    gather_w.take(12, 13, 14, 15)
    kv_sent = wall.at[:, :, pl.ds(pl.multiple_of(c * 640, 128), 128)]
    kv_came = wall.at[:, :, pl.ds(pl.multiple_of(other * 640, 128), 128)]
    message(M_SIB_KV, kv_sent, kv_sent, sibling).start()
    gather_o.take(0, 1, 4, 8)
    message(M_SIB_KV, kv_came, kv_came, None).wait_recv()

    def project(rel):
        zz = zr[rel]
        ref = x_rows(other, zz, 0, 256)
        message(M_SIB_X + (rel % 4), ref, ref, None).wait_recv()
        rows = pl.ds(pl.multiple_of(zz * 256, 256), 256)

        def columns(n, carry):
            cols = pl.ds(pl.multiple_of(n * 256, 256), 256)
            acc = jnp.dot(x_buf[0, rows, :], wall[0:8, :, cols].reshape(2048, 256), preferred_element_type=F32)
            acc += jnp.dot(x_buf[1, rows, :], wall[8:16, :, cols].reshape(2048, 256), preferred_element_type=F32)
            acc = jnp.transpose(acc.reshape(16, 2, 8, 256), (1, 0, 2, 3)).reshape(256, 256)
            qkv[rows, cols] = acc.astype(BF)
            return carry

        lax.fori_loop(0, 3, columns, 0)

    project(0)
    project(-1)
    gather_o.take(2, 3, 5, 10)
    project(1)
    for e in range(16):
        opposite(e)
    project(2)

    def attend(i, zz):
        def half_block(half, carry):
            qb = zz * 2 + half
            rows = pl.ds(pl.multiple_of(qb * 128, 128), 128)
            window = pl.ds(pl.multiple_of(jnp.maximum(qb - 4, 0) * 128, 128), 640)
            query = jnp.concatenate([qkv[rows, 128 + 128 * h : 256 + 128 * h] for h in range(4)], axis=0)
            keys, values = qkv[window, 0:128], qkv[window, 640:768]
            scores = lax.dot_general(query, keys, (((1,), (1,)), ((), ())), preferred_element_type=F32)
            scores = scores.reshape(4, 128, 640) + bias[qb][None]
            top = jnp.max(scores, axis=2, keepdims=True)
            weights = jnp.exp2((scores - top) * EXP_SCALE)
            total = jnp.sum(weights, axis=2, keepdims=True).reshape(512, 1)
            mixed = jnp.dot(weights.astype(BF).reshape(512, 640), values, preferred_element_type=F32) / total
            for h in range(4):
                ho[c, rows, 128 * h : 128 * h + 128] = mixed[128 * h : 128 * h + 128].astype(BF)
            return carry

        lax.fori_loop(0, 2, half_block, 0)
        rows = pl.ds(pl.multiple_of(zz * 256, 256), 256)
        message(M_SIB_HO + i, ho.at[c, rows, :], ho.at[c, rows, :], sibling).start()

    def project_out(i, zz, xs, half):
        rows = pl.ds(pl.multiple_of(zz * 256, 256), 256)
        cols = pl.ds(pl.multiple_of(xs * 256, 256), 256)
        lhs = jnp.concatenate([ho[0, rows, :], ho[1, rows, :]], axis=1)
        rhs = jnp.concatenate([wob[xs * 4 + half * 2], wob[xs * 4 + half * 2 + 1]], axis=1)
        acc = jnp.dot(lhs, rhs, preferred_element_type=F32)
        acc = jnp.transpose(acc.reshape(2, 16, 8, 256), (1, 0, 2, 3)).reshape(4, 64, 256)
        for row in range(4):
            kx = lax.rem(row - x + 4, 4)
            if i > 0:
                p32[i - 1, kx, half, :, cols] = acc[row]
            if i < 3:
                snd[i, kx, half, :, cols] = acc[row].astype(BF)

    def heads_of_sibling(i, zz):
        ref = ho.at[other, pl.ds(pl.multiple_of(zz * 256, 256), 256), :]
        message(M_SIB_HO + i, ref, ref, None).wait_recv()

    attend(0, zr[2])
    heads_of_sibling(0, zr[2])
    for q, dx in enumerate((0, -1, 1, 2)):
        if q == 0:
            gather_o.take(12, halves=(1,))
        elif q == 1:
            gather_o.take(11)
            gather_o.take(6, 7, halves=(0,))
            gather_o.take(9, 13, halves=(1,))
        elif q == 2:
            gather_o.take(9, halves=(0,))
            gather_o.take(6, 14, halves=(1,))
        else:
            gather_o.take(12, 13, 14, 15, halves=(0,))
            gather_o.take(7, 15, halves=(1,))

        def both(half, carry):
            project_out(0, zr[2], xr[dx], half)
            return carry

        lax.fori_loop(0, 2, both, 0)
        cols = pl.ds(pl.multiple_of(xr[dx] * 256, 256), 256)
        for half, dev in ((0, z_up), (1, z_down)):
            message(M_OPP + 2 * q + half, snd.at[0, :, half, :, cols], opr.at[half, :, :, cols], dev).start()

    def fin_message(side, kx, half):
        return message(
            M_FIN + 8 * side + 2 * kx + half, snd.at[1 + side, kx, half], fin.at[side, kx, half],
            z_down if side else z_up)

    def whole(i, zz):
        attend(i, zz)
        heads_of_sibling(i, zz)

        def both(n, carry):
            project_out(i, zz, lax.div(n, 2), lax.rem(n, 2))
            return carry

        lax.fori_loop(0, 8, both, 0)

    whole(1, zr[1])
    fin_message(0, 0, 1).start()
    fin_message(0, 1, 1).start()
    whole(2, zr[-1])
    fin_message(1, 0, 0).start()
    fin_message(1, 1, 0).start()
    for q, dx in enumerate((0, -1, 1, 2)):
        cols = pl.ds(pl.multiple_of(xr[dx] * 256, 256), 256)
        for half in range(2):
            ref = opr.at[half, :, :, cols]
            message(M_OPP + 2 * q + half, ref, ref, None).wait_recv()
    for kx in range(4):
        for side in range(2):
            snd[1 + side, kx, side] = (p32[side, kx, side] + opr[side, kx].astype(F32)).astype(BF)
            fin_message(side, kx, side).start()
            if kx < 2:
                fin_message(side, kx + 2, 1 - side).start()
    whole(3, z)

    for kx in range(4):
        for side in range(2):
            for half in range(2):
                fin_message(side, kx, half).wait_recv()

        def total(yy, carry):
            rows = pl.ds(pl.multiple_of(yy * 16, 16), 16)
            tot = [
                p32[2, kx, half, rows, :] + fin[0, kx, half, rows, :].astype(F32) + fin[1, kx, half, rows, :].astype(F32)
                for half in range(2)
            ]
            for core in range(2):
                fs[kx, yy, core] = jnp.concatenate([t[core * 8 : core * 8 + 8] for t in tot], axis=0).astype(BF)
            return carry

        lax.fori_loop(0, 4, total, 0)
        for ky in (2, 1, 3, 0):
            for kc in range(2):
                core = c if kc == 0 else other
                src, dst = fs.at[kx, yr[ky], core], r_buf.at[c, dp]
                if kx or ky or kc:
                    message(M_HOME + kx * 8 + ky * 2 + kc, src, dst, (plane(kx, ky), z * 2 + core)).start()
                else:
                    keep = pltpu.make_async_copy(src, dst, lsem.at[3])
                    keep.start()

    keep.wait()
    for kx in range(4):
        for ky in range(4):
            for kc in range(2):
                if kx or ky or kc:
                    ref = r_buf.at[c if kc == 0 else other, back(kx, ky)]
                    message(M_HOME + kx * 8 + ky * 2 + kc, ref, ref, None).wait_recv()

    for core in range(2):
        for h in range(2):
            rows = jnp.dot(pick[h], r_buf[core].reshape(256, 1024), preferred_element_type=F32).astype(BF)
            for i in range(8):
                at_col = (4 * (i // 2) + 2 * h + i % 2) * 256 + core * 128
                out[:, at_col : at_col + 128] = rows[:, i * 128 : i * 128 + 128]

    sib_rows.wait_send()
    sib_wo.wait_send()
    message(M_SIB_KV, kv_sent, kv_sent, None).wait_send()
    for rel in range(4):
        ref = x_rows(c, zr[rel], 0, 256)
        message(M_SIB_X + rel, ref, ref, None).wait_send()
        ref = ho.at[c, pl.ds(0, 256), :]
        message(M_SIB_HO + rel, ref, ref, None).wait_send()
    for k in range(1, 16):
        message(M_A2A + k, piece(dp), piece(dp), None).wait_send()
    for k in range(48):
        ref = x_rows(c, z, 0, 16)
        message(M_Z + k, ref, ref, None).wait_send()
    gather_w.drain()
    gather_o.drain()
    for k in range(8):
        message(M_OPP + k, snd.at[0, :, 0, :, pl.ds(0, 256)], opr.at[0, :, :, pl.ds(0, 256)], None).wait_send()
    for side in range(2):
        for kx in range(4):
            for half in range(2):
                fin_message(side, kx, half).wait_send()
    for k in range(1, 32):
        message(M_HOME + k, fs.at[0, 0, 0], r_buf.at[0, 0], None).wait_send()


def per_device(tokens, norm_gain, send_order, segment_ids, w_query, w_key, w_value, w_out):
    vmem = pl.BlockSpec(memory_space=pltpu.VMEM)
    hbm = pl.BlockSpec(memory_space=pl.ANY)
    return pl.pallas_call(
        kernel,
        out_shape=jax.ShapeDtypeStruct((128, 4096), BF),
        in_specs=[hbm] + [vmem] * 3 + [hbm] * 4,
        out_specs=vmem,
        scratch_shapes=[
            pltpu.VMEM((128, 4096), BF),
            pltpu.VMEM((2, 1024, 2048), BF),
            pltpu.VMEM((2, 128, 2048), BF),
            pltpu.VMEM((128, 2048), BF),
            pltpu.VMEM((256, 2048), BF),
            pltpu.VMEM((16, 256, 768), BF),
            pltpu.VMEM((16, 1024, 128), BF),
            pltpu.VMEM((1024, 768), BF),
            pltpu.VMEM((2, 1024, 512), BF),
            pltpu.VMEM((8, 128, 640), F32),
            pltpu.VMEM((3, 4, 2, 64, 1024), F32),
            pltpu.VMEM((3, 4, 2, 64, 1024), BF),
            pltpu.VMEM((2, 4, 64, 1024), BF),
            pltpu.VMEM((2, 4, 2, 64, 1024), BF),
            pltpu.VMEM((4, 4, 2, 16, 1024), BF),
            pltpu.VMEM((2, 16, 16, 1024), BF),
            pltpu.VMEM((2, 128, 256), BF),
            pltpu.SemaphoreType.DMA((6,)),
            pltpu.SemaphoreType.DMA((M_COUNT,)),
            pltpu.SemaphoreType.DMA((M_COUNT,)),
        ],
        compiler_params=pltpu.CompilerParams(
            collective_id=0, has_side_effects=True, vmem_limit_bytes=60 * 1024 * 1024
        ),
    )(tokens, norm_gain.reshape(1, 4096), send_order, segment_ids, w_query, w_key, w_value, w_out)


def solution(mesh):
    return jax.shard_map(
        per_device,
        mesh=mesh,
        in_specs=(
            P(("dp", "seq"), None),
            P(),
            P(("dp", "seq"), None),
            P("dp", None),
            P("dp", "seq"),
            P("dp", None),
            P("dp", None),
            P("seq", "dp"),
        ),
        out_specs=P(("dp", "seq"), None),
        check_vma=False,
    )
```

time: 136 us -> 130 us (0.956)
  Pallas kernels: 133 us -> 127 us
    pallas_call x1, Pallas kernels: 133 us -> 127 us  [per_device(): pl.pallas_call(kernel, out_shape=jax.ShapeDtypeStruct((128, 4096), BF), i...]
where the time goes in v2:
time: 130 us
  Pallas kernels  127 us (98%)
  local copies, waits for them, and re-layouts  2.29 us (2%)
    pallas_call x1, Pallas kernels, per_device(): pl.pallas_call(kernel, out_shape=jax.ShapeDtypeStruct((128, 4096), BF), i...  127 us

profile of v2, /device:TPU:1, one launch (start us, length us, event | category | flops | bytes accessed | tf_op | source)
XLA Modules:
  0.0 129.6 jit_solution(9399597351647014259)
XLA Ops:
  0.0 127.3 %shard_map.82 = bf16[128,4096]{1,0:T(8,128)(2,1)} custom-call(bf16[128,4096]{1,0:T(8,128)(2,1)} %tok_hbm.1, f32[1,4096]{1,0:T(1,128)} %bitcast.1, s32[1,128]{1,0:T(1,128)} %order.1, s32[1,1024]{1,0:T(1,128)} %seg.1, bf16[256,512]{1,0:T(8,128)(2,1)} %wq.1, bf16[256,512]{1,0:T(8,128)(2,1)} %wk.1, bf16[256,512]{1,0:T(8,128)(2,1)} %wv.1, bf16[512,256]{1,0:T(8,128)(2,1)} %wo.1), custom_call_target="tpu_custom_call" | custom-call | tf_op jit(solution)/shard_map/pallas_call | solution.py:493
  127.3 2.3 %copy.10 = bf16[128,4096]{1,0:T(8,128)(2,1)} copy(bf16[128,4096]{1,0:T(8,128)(2,1)} %shard_map.82) | data formatting | bytes 2097152

commit v3 on v2

v3 whole, which is shorter than its diff:
```python
import jax
import jax.numpy as jnp
from jax import lax
from jax.experimental import pallas as pl
from jax.experimental.pallas import tpu as pltpu
from jax.sharding import PartitionSpec as P

BF = jnp.bfloat16
F32 = jnp.float32
MESH = pl.DeviceIdType.MESH
NEG = float("-inf")
EXP_SCALE = 128 ** (-0.5) * 1.4426950408889634

M_SIB_ROWS = 0
M_SIB_WO = 1
M_SIB_KV = 2
M_SIB_X = 6
M_SIB_HO = 10
M_A2A = 18
M_Z = 34
M_W = 82
M_WO = 114
M_OPP = 146
M_FIN = 147
M_HOME = 151
M_COUNT = 152
S_SIB, S_WO_SIB, S_KV, S_X, S_HO, S_A2A, S_Z, S_W, S_WO, S_OPP, S_FIN, S_HOME, S_COUNT = range(13)

OFFSETS = (
    (0, 0), (1, 0), (3, 0), (0, 1), (0, 3), (2, 0), (0, 2), (1, 1), (3, 3), (1, 3), (3, 1),
    (2, 1), (2, 3), (1, 2), (3, 2), (2, 2),
)


class Gather:
    PLACE = {
        0: (-1, 0), 1: (1, 0), 2: (2, 0), 3: (2, 0), 4: (0, -1), 5: (-1, -1), 6: (1, -1), 7: (2, -1),
        8: (0, 1), 9: (-1, 1), 10: (1, 1), 11: (2, 1), 12: (0, 2), 13: (-1, 2), 14: (1, 2), 15: (2, 2),
    }
    ONWARD = {
        0: ((2, 1, 0), (5, 0, 1), (9, 0, -1)), 1: ((3, -1, 0), (6, 0, 1), (10, 0, -1)),
        3: ((7, 0, 1), (11, 0, -1)), 4: ((12, 0, 1),), 5: ((13, 0, 1),), 10: ((14, 0, -1),), 11: ((15, 0, -1),),
    }

    def __init__(self, base, group, view, rows, at, message):
        self.base, self.group, self.view, self.rows, self.at, self.message = base, group, view, rows, at, message

    def part(self, h, d1, d2, quarter=None):
        half = self.rows // 2
        if quarter is None:
            return self.view(self.at(h, d1, d2), h * half, half)
        return self.view(self.at(h, d1, d2), h * half + quarter * (half // 2), half // 2)

    def send(self, h, m, ref, d1, d2):
        self.message(self.base + 16 * h + m, self.group, ref, ref, (self.at(h, d1, d2), None)).start()

    def own(self):
        for h in range(2):
            mine = self.part(h, 0, 0)
            self.send(h, 0, mine, 1, 0)
            self.send(h, 1, mine, -1, 0)
            self.send(h, 4, mine, 0, 1)
            self.send(h, 8, mine, 0, -1)

    def take(self, *messages, halves=(0, 1)):
        for m in messages:
            for h in halves:
                d1, d2 = self.PLACE[m]
                ref = self.part(h, d1, d2, m - 2 if m in (2, 3) else None)
                self.message(self.base + 16 * h + m, self.group, ref, ref, None).wait_recv()
                for then, s1, s2 in self.ONWARD.get(m, ()):
                    self.send(h, then, self.part(h, d1, d2, then - 2 if then in (2, 3) else None), s1, s2)


def kernel(
    tok, gain, order, seg, wq, wk, wv, wo, out,
    x_buf, nb, sib, s_buf, wall, wob, qkv, ho, bias, p32, snd, opr, fin, fs, r_buf, pick, part,
    lsem, ssem, rsem,
):
    dp = lax.axis_index("dp")
    sq = lax.axis_index("seq")
    x, y = lax.div(dp, 4), lax.rem(dp, 4)
    z, c = lax.div(sq, 2), lax.rem(sq, 2)
    other = 1 - c

    def ring(v):
        return {0: v, 1: lax.rem(v + 1, 4), 2: lax.rem(v + 2, 4), -1: lax.rem(v + 3, 4), 3: lax.rem(v + 3, 4)}

    xr, yr, zr = ring(x), ring(y), ring(z)

    def plane(kx, ky):
        return xr[kx] * 4 + yr[ky]

    def back(kx, ky):
        return xr[(4 - kx) % 4] * 4 + yr[(4 - ky) % 4]

    def message(index, group, src, dst, dev):
        if dev is None:
            dev = (dp, z * 2 + other)
        elif dev[1] is None:
            dev = (dev[0], sq)
        return pltpu.make_async_remote_copy(
            src_ref=src, dst_ref=dst, send_sem=ssem.at[group], recv_sem=rsem.at[index],
            device_id=dev, device_id_type=MESH,
        )

    sibling = (dp, z * 2 + other)
    z_up, z_down = (dp, zr[1] * 2 + c), (dp, zr[-1] * 2 + c)

    barrier = pltpu.get_barrier_semaphore()
    greeted = [sibling, z_up, z_down]
    for kx in range(4):
        for ky in range(4):
            if kx or ky:
                greeted.append((plane(kx, ky), sq))
                greeted.append((plane(kx, ky), z * 2 + other))
    for dev in greeted:
        pl.semaphore_signal(barrier, inc=1, device_id=dev, device_id_type=MESH)

    load_q = pltpu.make_async_copy(wq, wall.at[dp, :, pl.ds(128, 512)], lsem.at[0])
    load_q.start()
    load_o = pltpu.make_async_copy(
        wo.at[:, pl.ds(pl.multiple_of(c * 128, 128), 128)],
        wob.at[dp, pl.ds(pl.multiple_of(c * 512, 512), 512), :], lsem.at[2])
    load_o.start()
    kv_cols = pl.ds(pl.multiple_of(z * 128, 128), 128)
    load_k = pltpu.make_async_copy(wk.at[:, kv_cols], wall.at[dp, :, pl.ds(0, 128)], lsem.at[1])
    load_v = pltpu.make_async_copy(wv.at[:, kv_cols], wall.at[dp, :, pl.ds(640, 128)], lsem.at[1])

    @pl.when(c == 0)
    def _():
        load_k.start()

    @pl.when(c == 1)
    def _():
        load_v.start()

    def norm_rows(i, carry):
        rows = pl.ds(pl.multiple_of(i * 16, 16), 16)
        wide = tok[rows, :].astype(F32)
        square = jnp.mean(wide * wide, axis=1, keepdims=True)
        out[rows, :] = (wide * lax.rsqrt(square + 1e-05) * gain[...]).astype(BF)
        return carry

    lax.fori_loop(0, 8, norm_rows, 0)

    to_home = (order[...] == lax.broadcasted_iota(jnp.int32, (128, 128), 0)).astype(F32)
    to_send = to_home.T.astype(BF)

    def permute(i, carry):
        half, k = lax.div(i, 4), lax.rem(i, 4)
        nb[half, :, pl.ds(pl.multiple_of(k * 512, 512), 512)] = jnp.dot(
            to_send, out[:, pl.ds(pl.multiple_of(i * 512, 512), 512)], preferred_element_type=F32
        ).astype(BF)
        return carry

    lax.fori_loop(0, 8, permute, 0)

    column = lax.broadcasted_iota(jnp.int32, (128, 256), 1)
    source = lax.div(column, 16) * 8 + lax.rem(column, 8)
    for h in range(2):
        spread = (lax.broadcasted_iota(jnp.int32, (128, 256), 0) == source) & (lax.rem(lax.div(column, 8), 2) == h)
        pick[h] = jnp.dot(to_home.astype(BF), spread.astype(F32).astype(BF), preferred_element_type=F32).astype(BF)

    def mask_rows(qb, carry):
        seg_q = seg[:, pl.ds(pl.multiple_of(qb * 128, 128), 128)].astype(F32)
        seg_q = jnp.broadcast_to(seg_q, (128, 128)).T
        start = jnp.maximum(qb - 4, 0) * 128
        row_at = qb * 128 + lax.broadcasted_iota(jnp.int32, (128, 128), 0)
        for k in range(5):
            seg_k = seg[:, pl.ds(pl.multiple_of(start + k * 128, 128), 128)].astype(F32)
            col_at = start + k * 128 + lax.broadcasted_iota(jnp.int32, (128, 128), 1)
            visible = (seg_q == seg_k) & (row_at >= col_at)
            bias[qb, :, k * 128 : (k + 1) * 128] = jnp.where(visible, 0.0, NEG)
        return carry

    lax.fori_loop(0, 8, mask_rows, 0)

    @pl.when(c == 0)
    def _():
        load_k.wait()

    @pl.when(c == 1)
    def _():
        load_v.wait()

    load_q.wait()
    pl.semaphore_wait(barrier, len(greeted))

    def at(h, d1, d2):
        return xr[d2] * 4 + yr[d1] if h == 0 else xr[d1] * 4 + yr[d2]

    sib_rows = message(M_SIB_ROWS, S_SIB, nb.at[other], sib, sibling)
    sib_rows.start()
    own_cols = pl.ds(pl.multiple_of(c * 128, 128), 640)
    gather_w = Gather(M_W, S_W, lambda j, lo, n: wall.at[j, pl.ds(lo, n), own_cols], 256, at, message)
    gather_o = Gather(M_WO, S_WO, lambda j, lo, n: wob.at[j, pl.ds(lo, n), :], 1024, at, message)
    gather_w.own()
    sib_rows.wait_recv()

    def interleave(i, carry):
        cols = pl.ds(pl.multiple_of(i * 256, 256), 256)
        mine = nb[c, :, cols].astype(F32)
        his = sib[:, cols].astype(F32)
        low = jnp.where(c == 0, mine, his).reshape(16, 1, 8, 256)
        high = jnp.where(c == 0, his, mine).reshape(16, 1, 8, 256)
        s_buf[:, cols] = jnp.concatenate([low, high], axis=1).reshape(256, 256).astype(BF)
        return carry

    lax.fori_loop(0, 8, interleave, 0)

    def x_rows(half, zz, row, count):
        return x_buf.at[half, pl.ds(pl.multiple_of(zz * 256 + row, 16), count), :]

    def piece(j):
        return s_buf.at[pl.ds(pl.multiple_of(j * 16, 16), 16), :]

    for kx, ky in OFFSETS[1:]:
        j = plane(kx, ky)
        message(M_A2A + kx * 4 + ky, S_A2A, piece(j), x_rows(c, z, dp * 16, 16), (j, sq)).start()
    x_buf[c, pl.ds(pl.multiple_of(z * 256 + dp * 16, 16), 16), :] = s_buf[pl.ds(pl.multiple_of(dp * 16, 16), 16), :]

    def to_sibling(rel, row):
        ref = x_rows(c, zr[rel], row, 16)
        message(M_SIB_X + (rel % 4), S_X, ref, ref, sibling).start()

    def arrived(e):
        kx, ky = OFFSETS[e]
        row = back(kx, ky) * 16
        ref = x_rows(c, z, row, 16)
        if kx or ky:
            message(M_A2A + kx * 4 + ky, S_A2A, ref, ref, None).wait_recv()
        message(M_Z + e, S_Z, ref, ref, z_up).start()
        message(M_Z + 16 + e, S_Z, ref, ref, z_down).start()
        to_sibling(0, row)

    def passed(e):
        row = back(*OFFSETS[e]) * 16
        low = x_rows(c, zr[-1], row, 16)
        message(M_Z + e, S_Z, low, low, None).wait_recv()
        if e % 2 == 0:
            message(M_Z + 32 + e, S_Z, low, low, z_up).start()
        to_sibling(-1, row)
        high = x_rows(c, zr[1], row, 16)
        message(M_Z + 16 + e, S_Z, high, high, None).wait_recv()
        if e % 2 == 1:
            message(M_Z + 32 + e, S_Z, high, high, z_down).start()
        to_sibling(1, row)

    def opposite(e):
        row = back(*OFFSETS[e]) * 16
        ref = x_rows(c, zr[2], row, 16)
        message(M_Z + 32 + e, S_Z, ref, ref, None).wait_recv()
        to_sibling(2, row)

    for e in range(7):
        arrived(e)
    wo_slot = wob.at[dp, pl.ds(pl.multiple_of(c * 512, 512), 512), :]
    sib_wo = message(
        M_SIB_WO, S_WO_SIB, wo.at[:, pl.ds(pl.multiple_of(other * 128, 128), 128)], wo_slot, sibling)
    sib_wo.start()
    gather_w.take(0, 1)
    for e in range(7, 11):
        arrived(e)
    gather_w.take(4, 8)
    for e in range(11, 16):
        arrived(e)
    gather_w.take(2, 3, 5, 10)
    for e in range(16):
        passed(e)
    gather_w.take(11)
    load_o.wait()
    sib_slot = wob.at[dp, pl.ds(pl.multiple_of(other * 512, 512), 512), :]
    message(M_SIB_WO, S_WO_SIB, sib_slot, sib_slot, None).wait_recv()
    gather_o.own()

    CHUNKS = (0, -1, 1, 2)

    def take_chunk(gather, q):
        if q == 0:
            gather.take(12, halves=(1,))
        elif q == 1:
            gather.take(6, 7, halves=(0,))
            gather.take(9, 13, halves=(1,))
        elif q == 2:
            gather.take(9, halves=(0,))
            gather.take(6, 14, halves=(1,))
        else:
            gather.take(12, 13, 14, 15, halves=(0,))
            gather.take(7, 15, halves=(1,))

    def kv_message(q, core):
        blocks = pl.ds(xr[CHUNKS[q]] * 4, 4)
        ref = wall.at[blocks, :, pl.ds(pl.multiple_of(core * 640, 128), 128)]
        return message(M_SIB_KV + q, S_KV, ref, ref, sibling)

    def sibling_rows(rel):
        ref = x_rows(other, zr[rel], 0, 256)
        message(M_SIB_X + (rel % 4), S_X, ref, ref, None).wait_recv()

    def store_qkv(rows, cols, acc):
        qkv[rows, cols] = jnp.transpose(acc.reshape(16, 2, 8, 256), (1, 0, 2, 3)).reshape(256, 256).astype(BF)

    def project_chunk(q):
        kv_message(q, other).wait_recv()
        xs = xr[CHUNKS[q]]
        features = pl.ds(pl.multiple_of(lax.rem(xs, 2) * 1024, 1024), 1024)
        blocks = pl.ds(xs * 4, 4)

        def columns(i, carry):
            k, n = lax.div(i, 3), lax.rem(i, 3)
            zz = lax.rem(z + k + lax.div(k, 2), 4)
            rows, cols = pl.ds(pl.multiple_of(zz * 256, 256), 256), pl.ds(pl.multiple_of(n * 256, 256), 256)
            acc = jnp.dot(
                x_buf[lax.div(xs, 2), rows, features], wall[blocks, :, cols].reshape(1024, 256),
                preferred_element_type=F32)
            if q > 0:
                acc += part[rows, cols]
            if q < 3:
                part[rows, cols] = acc
            else:
                store_qkv(rows, cols, acc)
            return carry

        lax.fori_loop(0, 9, columns, 0)

    take_chunk(gather_w, 0)
    kv_message(0, c).start()
    sibling_rows(0)
    sibling_rows(-1)
    sibling_rows(1)
    take_chunk(gather_w, 1)
    kv_message(1, c).start()
    project_chunk(0)
    take_chunk(gather_w, 2)
    kv_message(2, c).start()
    project_chunk(1)
    take_chunk(gather_w, 3)
    kv_message(3, c).start()
    project_chunk(2)
    for e in range(8):
        opposite(e)
    gather_o.take(0, 1, 4, 8)
    project_chunk(3)
    for e in range(8, 16):
        opposite(e)

    def project(rel):
        sibling_rows(rel)
        rows = pl.ds(pl.multiple_of(zr[rel] * 256, 256), 256)

        def columns(n, carry):
            cols = pl.ds(pl.multiple_of(n * 256, 256), 256)
            acc = jnp.dot(x_buf[0, rows, :], wall[0:8, :, cols].reshape(2048, 256), preferred_element_type=F32)
            acc += jnp.dot(x_buf[1, rows, :], wall[8:16, :, cols].reshape(2048, 256), preferred_element_type=F32)
            store_qkv(rows, cols, acc)
            return carry

        lax.fori_loop(0, 3, columns, 0)

    gather_o.take(2, 3)
    project(2)
    gather_o.take(5, 10)

    def attend(i, zz):
        def half_block(half, carry):
            qb = zz * 2 + half
            rows = pl.ds(pl.multiple_of(qb * 128, 128), 128)
            window = pl.ds(pl.multiple_of(jnp.maximum(qb - 4, 0) * 128, 128), 640)
            query = jnp.concatenate([qkv[rows, 128 + 128 * h : 256 + 128 * h] for h in range(4)], axis=0)
            keys, values = qkv[window, 0:128], qkv[window, 640:768]
            scores = lax.dot_general(query, keys, (((1,), (1,)), ((), ())), preferred_element_type=F32)
            scores = scores.reshape(4, 128, 640) + bias[qb][None]
            top = jnp.max(scores, axis=2, keepdims=True)
            weights = jnp.exp2((scores - top) * EXP_SCALE)
            total = jnp.sum(weights, axis=2, keepdims=True).reshape(512, 1)
            mixed = jnp.dot(weights.astype(BF).reshape(512, 640), values, preferred_element_type=F32) / total
            for h in range(4):
                ho[c, rows, 128 * h : 128 * h + 128] = mixed[128 * h : 128 * h + 128].astype(BF)
            message(M_SIB_HO + 2 * i + half, S_HO, ho.at[c, rows, :], ho.at[c, rows, :], sibling).start()
            return carry

        lax.fori_loop(0, 2, half_block, 0)

    def project_out(i, zz, xs, half):
        rows = pl.ds(pl.multiple_of(zz * 256, 256), 256)
        cols = pl.ds(pl.multiple_of(xs * 256, 256), 256)
        lhs = jnp.concatenate([ho[0, rows, :], ho[1, rows, :]], axis=1)
        rhs = jnp.concatenate([wob[xs * 4 + half * 2], wob[xs * 4 + half * 2 + 1]], axis=1)
        acc = jnp.dot(lhs, rhs, preferred_element_type=F32)
        acc = jnp.transpose(acc.reshape(2, 16, 8, 256), (1, 0, 2, 3)).reshape(4, 64, 256)
        for row in range(4):
            kx = lax.rem(row - x + 4, 4)
            if i > 0:
                p32[i - 1, kx, half, :, cols] = acc[row]
            if i < 3:
                snd[i, kx, half, :, cols] = acc[row].astype(BF)

    def heads_of_sibling(i, zz):
        for half in range(2):
            ref = ho.at[other, pl.ds(pl.multiple_of(zz * 256 + half * 128, 128), 128), :]
            message(M_SIB_HO + 2 * i + half, S_HO, ref, ref, None).wait_recv()

    def farthest(q):
        if q == 1:
            gather_o.take(11)
        take_chunk(gather_o, q)
        xs = xr[CHUNKS[q]]

        def both(half, carry):
            project_out(0, zr[2], xs, half)
            return carry

        lax.fori_loop(0, 2, both, 0)
        cols = pl.ds(pl.multiple_of(xs * 256, 256), 256)
        for half, dev in ((0, z_up), (1, z_down)):
            message(M_OPP, S_OPP, snd.at[0, :, half, :, cols], opr.at[half, :, :, cols], dev).start()

    def fin_message(side, kx, half):
        return message(
            M_FIN + kx, S_FIN, snd.at[1 + side, kx, half], fin.at[kx, side, half], z_down if side else z_up)

    def project_whole(i, zz):
        heads_of_sibling(i, zz)

        def both(n, carry):
            project_out(i, zz, lax.div(n, 2), lax.rem(n, 2))
            return carry

        lax.fori_loop(0, 8, both, 0)

    attend(0, zr[2])
    heads_of_sibling(0, zr[2])
    farthest(0)
    attend(1, zr[1])
    farthest(1)
    attend(2, zr[-1])
    farthest(2)
    farthest(3)
    project_whole(1, zr[1])
    fin_message(0, 0, 1).start()
    fin_message(0, 1, 1).start()
    project_whole(2, zr[-1])
    fin_message(1, 0, 0).start()
    fin_message(1, 1, 0).start()
    message(M_OPP, S_OPP, opr, opr, None).wait_recv()
    for kx in range(4):
        for side in range(2):
            snd[1 + side, kx, side] = (p32[side, kx, side] + opr[side, kx].astype(F32)).astype(BF)
            fin_message(side, kx, side).start()
            if kx < 2:
                fin_message(side, kx + 2, 1 - side).start()
    attend(3, z)
    project_whole(3, z)

    for kx in range(4):
        message(M_FIN + kx, S_FIN, fin.at[kx], fin.at[kx], None).wait_recv()

        def total(yy, carry):
            rows = pl.ds(pl.multiple_of(yy * 16, 16), 16)
            tot = [
                p32[2, kx, half, rows, :] + fin[kx, 0, half, rows, :].astype(F32) + fin[kx, 1, half, rows, :].astype(F32)
                for half in range(2)
            ]
            for core in range(2):
                fs[kx * 8 + yy * 2 + core] = jnp.concatenate([t[core * 8 : core * 8 + 8] for t in tot], axis=0).astype(BF)
            return carry

        lax.fori_loop(0, 4, total, 0)
        for ky in (2, 1, 3, 0):
            for kc in range(2):
                core = c if kc == 0 else other
                src, dst = fs.at[kx * 8 + yr[ky] * 2 + core], r_buf.at[c * 16 + dp]
                if kx or ky or kc:
                    message(M_HOME, S_HOME, src, dst, (plane(kx, ky), z * 2 + core)).start()
                else:
                    keep = pltpu.make_async_copy(src, dst, lsem.at[3])
                    keep.start()

    keep.wait()
    came = r_buf.at[pl.ds(0, 31)]
    message(M_HOME, S_HOME, came, came, None).wait_recv()

    for core in range(2):
        for h in range(2):
            rows = jnp.dot(pick[h], r_buf[core * 16 : core * 16 + 16].reshape(256, 1024), preferred_element_type=F32).astype(BF)
            for i in range(8):
                at_col = (4 * (i // 2) + 2 * h + i % 2) * 256 + core * 128
                out[:, at_col : at_col + 128] = rows[:, i * 128 : i * 128 + 128]

    def sent(group, ref):
        message(0, group, ref, ref, None).wait_send()

    sent(S_SIB, sib)
    sent(S_WO_SIB, wo_slot)
    sent(S_KV, wall.at[:, :, pl.ds(0, 128)])
    sent(S_X, x_buf.at[0])
    sent(S_HO, ho.at[0])
    sent(S_A2A, s_buf.at[pl.ds(0, 240), :])
    sent(S_Z, x_buf.at[0, pl.ds(0, 768), :])
    sent(S_W, wall.at[pl.ds(0, 15), :, pl.ds(0, 640)])
    sent(S_WO, wob.at[pl.ds(0, 15)])
    sent(S_OPP, snd.at[0])
    sent(S_FIN, snd.at[pl.ds(1, 2)])
    sent(S_HOME, fs.at[pl.ds(0, 31)])


def per_device(tokens, norm_gain, send_order, segment_ids, w_query, w_key, w_value, w_out):
    vmem = pl.BlockSpec(memory_space=pltpu.VMEM)
    hbm = pl.BlockSpec(memory_space=pl.ANY)
    return pl.pallas_call(
        kernel,
        out_shape=jax.ShapeDtypeStruct((128, 4096), BF),
        in_specs=[vmem] * 4 + [hbm] * 4,
        out_specs=vmem,
        scratch_shapes=[
            pltpu.VMEM((2, 1024, 2048), BF),
            pltpu.VMEM((2, 128, 2048), BF),
            pltpu.VMEM((128, 2048), BF),
            pltpu.VMEM((256, 2048), BF),
            pltpu.VMEM((16, 256, 768), BF),
            pltpu.VMEM((16, 1024, 128), BF),
            pltpu.VMEM((1024, 768), BF),
            pltpu.VMEM((2, 1024, 512), BF),
            pltpu.VMEM((8, 128, 640), F32),
            pltpu.VMEM((3, 4, 2, 64, 1024), F32),
            pltpu.VMEM((3, 4, 2, 64, 1024), BF),
            pltpu.VMEM((2, 4, 64, 1024), BF),
            pltpu.VMEM((4, 2, 2, 64, 1024), BF),
            pltpu.VMEM((32, 16, 1024), BF),
            pltpu.VMEM((32, 16, 1024), BF),
            pltpu.VMEM((2, 128, 256), BF),
            pltpu.VMEM((1024, 768), F32),
            pltpu.SemaphoreType.DMA((4,)),
            pltpu.SemaphoreType.DMA((S_COUNT,)),
            pltpu.SemaphoreType.DMA((M_COUNT,)),
        ],
        compiler_params=pltpu.CompilerParams(
            collective_id=0, has_side_effects=True, vmem_limit_bytes=60 * 1024 * 1024
        ),
    )(tokens, norm_gain.reshape(1, 4096), send_order, segment_ids, w_query, w_key, w_value, w_out)


def solution(mesh):
    return jax.shard_map(
        per_device,
        mesh=mesh,
        in_specs=(
            P(("dp", "seq"), None),
            P(),
            P(("dp", "seq"), None),
            P("dp", None),
            P("dp", "seq"),
            P("dp", None),
            P("dp", None),
            P("seq", "dp"),
        ),
        out_specs=P(("dp", "seq"), None),
        check_vma=False,
    )
```

time: 130 us -> 128 us (0.985)
  Pallas kernels: 127 us -> 125 us
    pallas_call x1, Pallas kernels: 127 us -> 125 us  [per_device(): pl.pallas_call(kernel, out_shape=jax.ShapeDtypeStruct((128, 4096), BF), i...]
where the time goes in v3:
time: 128 us; the launch traced here: 127 us
  Pallas kernels  125 us (98%)
  local copies, waits for them, and re-layouts  2.29 us (2%)
    pallas_call x1, Pallas kernels, per_device(): pl.pallas_call(kernel, out_shape=jax.ShapeDtypeStruct((128, 4096), BF), i...  125 us

profile of v3, /device:TPU:1, one launch (start us, length us, event | category | flops | bytes accessed | tf_op | source)
XLA Modules:
  0.0 126.9 jit_solution(2722996237495426061)
XLA Ops:
  0.0 124.6 %shard_map.82 = bf16[128,4096]{1,0:T(8,128)(2,1)} custom-call(bf16[128,4096]{1,0:T(8,128)(2,1)} %tok.1, f32[1,4096]{1,0:T(1,128)} %bitcast.1, s32[1,128]{1,0:T(1,128)} %order.1, s32[1,1024]{1,0:T(1,128)} %seg.1, bf16[256,512]{1,0:T(8,128)(2,1)} %wq.1, bf16[256,512]{1,0:T(8,128)(2,1)} %wk.1, bf16[256,512]{1,0:T(8,128)(2,1)} %wv.1, bf16[512,256]{1,0:T(8,128)(2,1)} %wo.1), custom_call_target="tpu_custom_call" | custom-call | tf_op jit(solution)/shard_map/pallas_call | solution.py:511
  124.6 2.3 %copy.10 = bf16[128,4096]{1,0:T(8,128)(2,1)} copy(bf16[128,4096]{1,0:T(8,128)(2,1)} %shard_map.82) | data formatting | bytes 2097152

commit v4 on v3

--- a/solution.py
+++ b/solution.py
@@ -195,7 +195,6 @@
     own_cols = pl.ds(pl.multiple_of(c * 128, 128), 640)
     gather_w = Gather(M_W, S_W, lambda j, lo, n: wall.at[j, pl.ds(lo, n), own_cols], 256, at, message)
     gather_o = Gather(M_WO, S_WO, lambda j, lo, n: wob.at[j, pl.ds(lo, n), :], 1024, at, message)
-    gather_w.own()
     sib_rows.wait_recv()
 
     def interleave(i, carry):
@@ -215,9 +214,12 @@
     def piece(j):
         return s_buf.at[pl.ds(pl.multiple_of(j * 16, 16), 16), :]
 
-    for kx, ky in OFFSETS[1:]:
-        j = plane(kx, ky)
-        message(M_A2A + kx * 4 + ky, S_A2A, piece(j), x_rows(c, z, dp * 16, 16), (j, sq)).start()
+    def scatter(first, last):
+        for kx, ky in OFFSETS[first:last]:
+            j = plane(kx, ky)
+            message(M_A2A + kx * 4 + ky, S_A2A, piece(j), x_rows(c, z, dp * 16, 16), (j, sq)).start()
+
+    scatter(1, 7)
     x_buf[c, pl.ds(pl.multiple_of(z * 256 + dp * 16, 16), 16), :] = s_buf[pl.ds(pl.multiple_of(dp * 16, 16), 16), :]
 
     def to_sibling(rel, row):
@@ -253,26 +255,96 @@
         message(M_Z + 32 + e, S_Z, ref, ref, None).wait_recv()
         to_sibling(2, row)
 
-    for e in range(7):
+    arrived(0)
+    gather_w.own()
+    for e in range(1, 5):
         arrived(e)
+    scatter(7, 11)
     wo_slot = wob.at[dp, pl.ds(pl.multiple_of(c * 512, 512), 512), :]
     sib_wo = message(
         M_SIB_WO, S_WO_SIB, wo.at[:, pl.ds(pl.multiple_of(other * 128, 128), 128)], wo_slot, sibling)
     sib_wo.start()
+    for e in range(5, 7):
+        arrived(e)
+    scatter(11, 16)
     gather_w.take(0, 1)
     for e in range(7, 11):
         arrived(e)
     gather_w.take(4, 8)
     for e in range(11, 16):
         arrived(e)
+
+    GROUPS = (
+        ((0, 0), (0, 1), (0, -1), (1, 0), (-1, 0)),
+        ((0, 2), (2, 0), (1, 1), (1, -1), (-1, 1), (-1, -1)),
+        ((2, 1), (2, -1), (1, 2), (-1, 2), (2, 2)),
+    )
+
+    def kv_send(q):
+        cols = pl.ds(pl.multiple_of(c * 640, 128), 128)
+        for kx, ky in GROUPS[q]:
+            ref = wall.at[plane(kx, ky), :, cols]
+            message(M_SIB_KV + q, S_KV, ref, ref, sibling).start()
+
+    def kv_wait(q):
+        ref = wall.at[pl.ds(0, len(GROUPS[q])), :, pl.ds(pl.multiple_of(other * 640, 128), 128)]
+        message(M_SIB_KV + q, S_KV, ref, ref, None).wait_recv()
+
+    def sibling_rows(rel):
+        ref = x_rows(other, zr[rel], 0, 256)
+        message(M_SIB_X + (rel % 4), S_X, ref, ref, None).wait_recv()
+
+    def project(q, first, last):
+        blocks = [plane(kx, ky) for kx, ky in GROUPS[q]]
+
+        def columns(i, carry):
+            k, n = lax.div(i, 3), lax.rem(i, 3)
+            zz = lax.rem(z + k + lax.div(k, 2) - 2 * lax.div(k, 3), 4)
+            rows, cols = pl.ds(pl.multiple_of(zz * 256, 256), 256), pl.ds(pl.multiple_of(n * 256, 256), 256)
+            acc = part[rows, cols] if q > 0 else 0.0
+            for j in blocks:
+                features = pl.ds(pl.multiple_of(lax.rem(j, 8) * 256, 256), 256)
+                acc += jnp.dot(x_buf[lax.div(j, 8), rows, features], wall[j, :, cols], preferred_element_type=F32)
+            if q < 2:
+                part[rows, cols] = acc
+            else:
+                acc = jnp.transpose(acc.reshape(16, 2, 8, 256), (1, 0, 2, 3)).reshape(256, 256)
+                qkv[rows, cols] = acc.astype(BF)
+            return carry
+
+        lax.fori_loop(3 * first, 3 * last, columns, 0)
+
     gather_w.take(2, 3, 5, 10)
-    for e in range(16):
+    kv_send(0)
+    for e in range(8):
         passed(e)
-    gather_w.take(11)
+    sibling_rows(0)
+    kv_wait(0)
+    project(0, 0, 1)
+    for e in range(8, 16):
+        passed(e)
+    gather_w.take(12, 6, 9, 11)
+    kv_send(1)
     load_o.wait()
     sib_slot = wob.at[dp, pl.ds(pl.multiple_of(other * 512, 512), 512), :]
     message(M_SIB_WO, S_WO_SIB, sib_slot, sib_slot, None).wait_recv()
     gather_o.own()
+    sibling_rows(1)
+    sibling_rows(-1)
+    project(0, 1, 3)
+    kv_wait(1)
+    project(1, 0, 3)
+    for e in range(16):
+        opposite(e)
+    gather_w.take(7, 13, 14, 15)
+    kv_send(2)
+    sibling_rows(2)
+    project(0, 3, 4)
+    project(1, 3, 4)
+    kv_wait(2)
+    gather_o.take(0, 1, 4, 8)
+    project(2, 0, 4)
+    gather_o.take(2, 3, 5, 10)
 
     CHUNKS = (0, -1, 1, 2)
 
@@ -288,79 +360,6 @@
         else:
             gather.take(12, 13, 14, 15, halves=(0,))
             gather.take(7, 15, halves=(1,))
-
-    def kv_message(q, core):
-        blocks = pl.ds(xr[CHUNKS[q]] * 4, 4)
-        ref = wall.at[blocks, :, pl.ds(pl.multiple_of(core * 640, 128), 128)]
-        return message(M_SIB_KV + q, S_KV, ref, ref, sibling)
-
-    def sibling_rows(rel):
-        ref = x_rows(other, zr[rel], 0, 256)
-        message(M_SIB_X + (rel % 4), S_X, ref, ref, None).wait_recv()
-
-    def store_qkv(rows, cols, acc):
-        qkv[rows, cols] = jnp.transpose(acc.reshape(16, 2, 8, 256), (1, 0, 2, 3)).reshape(256, 256).astype(BF)
-
-    def project_chunk(q):
-        kv_message(q, other).wait_recv()
-        xs = xr[CHUNKS[q]]
-        features = pl.ds(pl.multiple_of(lax.rem(xs, 2) * 1024, 1024), 1024)
-        blocks = pl.ds(xs * 4, 4)
-
-        def columns(i, carry):
-            k, n = lax.div(i, 3), lax.rem(i, 3)
-            zz = lax.rem(z + k + lax.div(k, 2), 4)
-            rows, cols = pl.ds(pl.multiple_of(zz * 256, 256), 256), pl.ds(pl.multiple_of(n * 256, 256), 256)
-            acc = jnp.dot(
-                x_buf[lax.div(xs, 2), rows, features], wall[blocks, :, cols].reshape(1024, 256),
-                preferred_element_type=F32)
-            if q > 0:
-                acc += part[rows, cols]
-            if q < 3:
-                part[rows, cols] = acc
-            else:
-                store_qkv(rows, cols, acc)
-            return carry
-
-        lax.fori_loop(0, 9, columns, 0)
-
-    take_chunk(gather_w, 0)
-    kv_message(0, c).start()
-    sibling_rows(0)
-    sibling_rows(-1)
-    sibling_rows(1)
-    take_chunk(gather_w, 1)
-    kv_message(1, c).start()
-    project_chunk(0)
-    take_chunk(gather_w, 2)
-    kv_message(2, c).start()
-    project_chunk(1)
-    take_chunk(gather_w, 3)
-    kv_message(3, c).start()
-    project_chunk(2)
-    for e in range(8):
-        opposite(e)
-    gather_o.take(0, 1, 4, 8)
-    project_chunk(3)
-    for e in range(8, 16):
-        opposite(e)
-
-    def project(rel):
-        sibling_rows(rel)
-        rows = pl.ds(pl.multiple_of(zr[rel] * 256, 256), 256)
-
-        def columns(n, carry):
-            cols = pl.ds(pl.multiple_of(n * 256, 256), 256)
-            acc = jnp.dot(x_buf[0, rows, :], wall[0:8, :, cols].reshape(2048, 256), preferred_element_type=F32)
-            acc += jnp.dot(x_buf[1, rows, :], wall[8:16, :, cols].reshape(2048, 256), preferred_element_type=F32)
-            store_qkv(rows, cols, acc)
-            return carry
-
-        lax.fori_loop(0, 3, columns, 0)
-
-    gather_o.take(2, 3)
-    project(2)
-    gather_o.take(5, 10)
 
     def attend(i, zz):
         def half_block(half, carry):
@@ -388,13 +387,14 @@
         lhs = jnp.concatenate([ho[0, rows, :], ho[1, rows, :]], axis=1)
         rhs = jnp.concatenate([wob[xs * 4 + half * 2], wob[xs * 4 + half * 2 + 1]], axis=1)
         acc = jnp.dot(lhs, rhs, preferred_element_type=F32)
-        acc = jnp.transpose(acc.reshape(2, 16, 8, 256), (1, 0, 2, 3)).reshape(4, 64, 256)
-        for row in range(4):
-            kx = lax.rem(row - x + 4, 4)
+        acc = jnp.transpose(acc.reshape(2, 16, 8, 256), (1, 0, 2, 3)).reshape(16, 16, 256)
+        for j in range(16):
+            kx, ky = lax.rem(j // 4 - x + 4, 4), lax.rem(j % 4 - y + 4, 4)
+            group, at_row = lax.rem(ky - kx + 4, 4), pl.ds(pl.multiple_of(kx * 16, 16), 16)
             if i > 0:
-                p32[i - 1, kx, half, :, cols] = acc[row]
+                p32[i - 1, group, half, at_row, cols] = acc[j]
             if i < 3:
-                snd[i, kx, half, :, cols] = acc[row].astype(BF)
+                snd[i, group, half, at_row, cols] = acc[j].astype(BF)
 
     def heads_of_sibling(i, zz):
         for half in range(2):
@@ -416,9 +416,10 @@
         for half, dev in ((0, z_up), (1, z_down)):
             message(M_OPP, S_OPP, snd.at[0, :, half, :, cols], opr.at[half, :, :, cols], dev).start()
 
-    def fin_message(side, kx, half):
+    def fin_message(side, group, half):
         return message(
-            M_FIN + kx, S_FIN, snd.at[1 + side, kx, half], fin.at[kx, side, half], z_down if side else z_up)
+            M_FIN + group, S_FIN, snd.at[1 + side, group, half], fin.at[group, side, half],
+            z_down if side else z_up)
 
     def project_whole(i, zz):
         heads_of_sibling(i, zz)
@@ -444,35 +445,37 @@
     fin_message(1, 0, 0).start()
     fin_message(1, 1, 0).start()
     message(M_OPP, S_OPP, opr, opr, None).wait_recv()
-    for kx in range(4):
+    for group in range(4):
         for side in range(2):
-            snd[1 + side, kx, side] = (p32[side, kx, side] + opr[side, kx].astype(F32)).astype(BF)
-            fin_message(side, kx, side).start()
-            if kx < 2:
-                fin_message(side, kx + 2, 1 - side).start()
+            snd[1 + side, group, side] = (p32[side, group, side] + opr[side, group].astype(F32)).astype(BF)
+            fin_message(side, group, side).start()
+            if group < 2:
+                fin_message(side, group + 2, 1 - side).start()
     attend(3, z)
     project_whole(3, z)
 
-    for kx in range(4):
-        message(M_FIN + kx, S_FIN, fin.at[kx], fin.at[kx], None).wait_recv()
-
-        def total(yy, carry):
-            rows = pl.ds(pl.multiple_of(yy * 16, 16), 16)
+    for group in range(4):
+        message(M_FIN + group, S_FIN, fin.at[group], fin.at[group], None).wait_recv()
+
+        def total(k, carry):
+            rows = pl.ds(pl.multiple_of(k * 16, 16), 16)
             tot = [
-                p32[2, kx, half, rows, :] + fin[kx, 0, half, rows, :].astype(F32) + fin[kx, 1, half, rows, :].astype(F32)
+                p32[2, group, half, rows, :] + fin[group, 0, half, rows, :].astype(F32)
+                + fin[group, 1, half, rows, :].astype(F32)
                 for half in range(2)
             ]
             for core in range(2):
-                fs[kx * 8 + yy * 2 + core] = jnp.concatenate([t[core * 8 : core * 8 + 8] for t in tot], axis=0).astype(BF)
+                fs[group * 8 + k * 2 + core] = jnp.concatenate(
+                    [t[core * 8 : core * 8 + 8] for t in tot], axis=0).astype(BF)
             return carry
 
         lax.fori_loop(0, 4, total, 0)
-        for ky in (2, 1, 3, 0):
-            for kc in range(2):
-                core = c if kc == 0 else other
-                src, dst = fs.at[kx * 8 + yr[ky] * 2 + core], r_buf.at[c * 16 + dp]
-                if kx or ky or kc:
-                    message(M_HOME, S_HOME, src, dst, (plane(kx, ky), z * 2 + core)).start()
+        for k in (2, 1, 3, 0):
+            for same in range(2):
+                core = other if same == 0 else c
+                src, dst = fs.at[group * 8 + k * 2 + core], r_buf.at[c * 16 + dp]
+                if group or k or same == 0:
+                    message(M_HOME, S_HOME, src, dst, (plane(k, (k + group) % 4), z * 2 + core)).start()
                 else:
                     keep = pltpu.make_async_copy(src, dst, lsem.at[3])
                     keep.start()

time: 128 us -> 122 us (0.953)
  Pallas kernels: 125 us -> 120 us
    pallas_call x1, Pallas kernels: 125 us -> 120 us  [per_device(): pl.pallas_call(kernel, out_shape=jax.ShapeDtypeStruct((128, 4096), BF), i...]
where the time goes in v4:
time: 122 us
  Pallas kernels  120 us (98%)
  local copies, waits for them, and re-layouts  2.29 us (2%)
    pallas_call x1, Pallas kernels, per_device(): pl.pallas_call(kernel, out_shape=jax.ShapeDtypeStruct((128, 4096), BF), i...  120 us

profile of v4, /device:TPU:1, one launch (start us, length us, event | category | flops | bytes accessed | tf_op | source)
XLA Modules:
  0.0 121.9 jit_solution(5317453015555541877)
XLA Ops:
  0.0 119.6 %shard_map.82 = bf16[128,4096]{1,0:T(8,128)(2,1)} custom-call(bf16[128,4096]{1,0:T(8,128)(2,1)} %tok.1, f32[1,4096]{1,0:T(1,128)} %bitcast.1, s32[1,128]{1,0:T(1,128)} %order.1, s32[1,1024]{1,0:T(1,128)} %seg.1, bf16[256,512]{1,0:T(8,128)(2,1)} %wq.1, bf16[256,512]{1,0:T(8,128)(2,1)} %wk.1, bf16[256,512]{1,0:T(8,128)(2,1)} %wv.1, bf16[512,256]{1,0:T(8,128)(2,1)} %wo.1), custom_call_target="tpu_custom_call" | custom-call | tf_op jit(solution)/shard_map/pallas_call | solution.py:514
  119.6 2.3 %copy.10 = bf16[128,4096]{1,0:T(8,128)(2,1)} copy(bf16[128,4096]{1,0:T(8,128)(2,1)} %shard_map.82) | data formatting | bytes 2097152

commit v5 on v4

--- a/solution.py
+++ b/solution.py
@@ -54,8 +54,8 @@
     def send(self, h, m, ref, d1, d2):
         self.message(self.base + 16 * h + m, self.group, ref, ref, (self.at(h, d1, d2), None)).start()
 
-    def own(self):
-        for h in range(2):
+    def own(self, halves=(0, 1)):
+        for h in halves:
             mine = self.part(h, 0, 0)
             self.send(h, 0, mine, 1, 0)
             self.send(h, 1, mine, -1, 0)
@@ -94,6 +94,9 @@
     def back(kx, ky):
         return xr[(4 - kx) % 4] * 4 + yr[(4 - ky) % 4]
 
+    def half_of(kx, ky):
+        return lax.div(lax.rem(ky + 3 * lax.div(kx, 2), 4), 2)
+
     def message(index, group, src, dst, dev):
         if dev is None:
             dev = (dp, z * 2 + other)
@@ -158,9 +161,17 @@
 
     column = lax.broadcasted_iota(jnp.int32, (128, 256), 1)
     source = lax.div(column, 16) * 8 + lax.rem(column, 8)
-    for h in range(2):
-        spread = (lax.broadcasted_iota(jnp.int32, (128, 256), 0) == source) & (lax.rem(lax.div(column, 8), 2) == h)
-        pick[h] = jnp.dot(to_home.astype(BF), spread.astype(F32).astype(BF), preferred_element_type=F32).astype(BF)
+    spread = lax.broadcasted_iota(jnp.int32, (128, 256), 0) == source
+    whence = jnp.dot(to_home.astype(BF), spread.astype(F32).astype(BF), preferred_element_type=F32)
+    group_x, group_y = lax.div(column, 64), lax.rem(lax.div(column, 16), 4)
+    piece_half = lax.rem(lax.div(column, 8), 2)
+
+    def pick_block(j, carry):
+        here = half_of(lax.rem(lax.div(j, 4) - group_x + 4, 4), lax.rem(lax.rem(j, 4) - group_y + 4, 4))
+        pick[j] = jnp.where(here == piece_half, whence, 0.0).astype(BF)
+        return carry
+
+    lax.fori_loop(0, 16, pick_block, 0)
 
     def mask_rows(qb, carry):
         seg_q = seg[:, pl.ds(pl.multiple_of(qb * 128, 128), 128)].astype(F32)
@@ -195,6 +206,7 @@
     own_cols = pl.ds(pl.multiple_of(c * 128, 128), 640)
     gather_w = Gather(M_W, S_W, lambda j, lo, n: wall.at[j, pl.ds(lo, n), own_cols], 256, at, message)
     gather_o = Gather(M_WO, S_WO, lambda j, lo, n: wob.at[j, pl.ds(lo, n), :], 1024, at, message)
+    gather_w.own(halves=(0,))
     sib_rows.wait_recv()
 
     def interleave(i, carry):
@@ -256,7 +268,7 @@
         to_sibling(2, row)
 
     arrived(0)
-    gather_w.own()
+    gather_w.own(halves=(1,))
     for e in range(1, 5):
         arrived(e)
     scatter(7, 11)
@@ -336,30 +348,15 @@
     project(1, 0, 3)
     for e in range(16):
         opposite(e)
-    gather_w.take(7, 13, 14, 15)
-    kv_send(2)
     sibling_rows(2)
     project(0, 3, 4)
     project(1, 3, 4)
+    gather_w.take(7, 13, 14, 15)
+    kv_send(2)
+    gather_o.take(0, 1, 4, 8)
     kv_wait(2)
-    gather_o.take(0, 1, 4, 8)
     project(2, 0, 4)
     gather_o.take(2, 3, 5, 10)
-
-    CHUNKS = (0, -1, 1, 2)
-
-    def take_chunk(gather, q):
-        if q == 0:
-            gather.take(12, halves=(1,))
-        elif q == 1:
-            gather.take(6, 7, halves=(0,))
-            gather.take(9, 13, halves=(1,))
-        elif q == 2:
-            gather.take(9, halves=(0,))
-            gather.take(6, 14, halves=(1,))
-        else:
-            gather.take(12, 13, 14, 15, halves=(0,))
-            gather.take(7, 15, halves=(1,))
 
     def attend(i, zz):
         def half_block(half, carry):
@@ -381,40 +378,42 @@
 
         lax.fori_loop(0, 2, half_block, 0)
 
-    def project_out(i, zz, xs, half):
+    def project_out(i, zz, blocks):
         rows = pl.ds(pl.multiple_of(zz * 256, 256), 256)
-        cols = pl.ds(pl.multiple_of(xs * 256, 256), 256)
         lhs = jnp.concatenate([ho[0, rows, :], ho[1, rows, :]], axis=1)
-        rhs = jnp.concatenate([wob[xs * 4 + half * 2], wob[xs * 4 + half * 2 + 1]], axis=1)
-        acc = jnp.dot(lhs, rhs, preferred_element_type=F32)
-        acc = jnp.transpose(acc.reshape(2, 16, 8, 256), (1, 0, 2, 3)).reshape(16, 16, 256)
-        for j in range(16):
-            kx, ky = lax.rem(j // 4 - x + 4, 4), lax.rem(j % 4 - y + 4, 4)
-            group, at_row = lax.rem(ky - kx + 4, 4), pl.ds(pl.multiple_of(kx * 16, 16), 16)
-            if i > 0:
-                p32[i - 1, group, half, at_row, cols] = acc[j]
-            if i < 3:
-                snd[i, group, half, at_row, cols] = acc[j].astype(BF)
+        rhs = [wob[j] for j in blocks]
+        acc = jnp.dot(lhs, rhs[0] if len(rhs) == 1 else jnp.concatenate(rhs, axis=1), preferred_element_type=F32)
+        acc = jnp.transpose(acc.reshape(2, 16, 8, 128 * len(blocks)), (1, 0, 2, 3)).reshape(16, 16, 128 * len(blocks))
+        for n, j in enumerate(blocks):
+            bx, by = lax.div(j, 4), lax.rem(j, 4)
+            half = half_of(lax.rem(bx - x + 4, 4), lax.rem(by - y + 4, 4))
+            cols = pl.ds(pl.multiple_of((bx * 2 + lax.rem(by, 2)) * 128, 128), 128)
+            for at_j in range(16):
+                kx, ky = lax.rem(at_j // 4 - x + 4, 4), lax.rem(at_j % 4 - y + 4, 4)
+                group, at_row = lax.rem(ky - kx + 4, 4), pl.ds(pl.multiple_of(kx * 16, 16), 16)
+                val = acc[at_j, :, 128 * n : 128 * n + 128]
+                if i > 0:
+                    p32[i - 1, group, half, at_row, cols] = val
+                if i < 3:
+                    snd[i, group, half, at_row, cols] = val.astype(BF)
 
     def heads_of_sibling(i, zz):
         for half in range(2):
             ref = ho.at[other, pl.ds(pl.multiple_of(zz * 256 + half * 128, 128), 128), :]
             message(M_SIB_HO + 2 * i + half, S_HO, ref, ref, None).wait_recv()
 
+    HALF = lambda kx, ky: ((ky % 4 + 3 * (kx % 4 // 2)) % 4) // 2
+
     def farthest(q):
-        if q == 1:
-            gather_o.take(11)
-        take_chunk(gather_o, q)
-        xs = xr[CHUNKS[q]]
-
-        def both(half, carry):
-            project_out(0, zr[2], xs, half)
-            return carry
-
-        lax.fori_loop(0, 2, both, 0)
-        cols = pl.ds(pl.multiple_of(xs * 256, 256), 256)
-        for half, dev in ((0, z_up), (1, z_down)):
-            message(M_OPP, S_OPP, snd.at[0, :, half, :, cols], opr.at[half, :, :, cols], dev).start()
+        offsets = GROUPS[q]
+        for first in range(0, len(offsets), 2):
+            project_out(0, zr[2], [plane(kx, ky) for kx, ky in offsets[first : first + 2]])
+            for kx, ky in offsets[first : first + 2]:
+                half, place = HALF(kx, ky), xr[kx] * 2 + lax.rem(yr[ky], 2)
+                cols = pl.ds(pl.multiple_of(place * 128, 128), 128)
+                message(
+                    M_OPP, S_OPP, snd.at[0, :, half, :, cols], opr.at[half, :, :, cols],
+                    z_down if half else z_up).start()
 
     def fin_message(side, group, half):
         return message(
@@ -425,7 +424,8 @@
         heads_of_sibling(i, zz)
 
         def both(n, carry):
-            project_out(i, zz, lax.div(n, 2), lax.rem(n, 2))
+            j = lax.div(n, 2) * 4 + lax.rem(n, 2)
+            project_out(i, zz, [j, j + 2])
             return carry
 
         lax.fori_loop(0, 8, both, 0)
@@ -433,11 +433,13 @@
     attend(0, zr[2])
     heads_of_sibling(0, zr[2])
     farthest(0)
+    gather_o.take(12, 6, 9)
+    farthest(1)
+    gather_o.take(11)
     attend(1, zr[1])
-    farthest(1)
+    gather_o.take(7, 13, 14, 15)
+    farthest(2)
     attend(2, zr[-1])
-    farthest(2)
-    farthest(3)
     project_whole(1, zr[1])
     fin_message(0, 0, 1).start()
     fin_message(0, 1, 1).start()
@@ -484,12 +486,11 @@
     came = r_buf.at[pl.ds(0, 31)]
     message(M_HOME, S_HOME, came, came, None).wait_recv()
 
-    for core in range(2):
-        for h in range(2):
-            rows = jnp.dot(pick[h], r_buf[core * 16 : core * 16 + 16].reshape(256, 1024), preferred_element_type=F32).astype(BF)
-            for i in range(8):
-                at_col = (4 * (i // 2) + 2 * h + i % 2) * 256 + core * 128
-                out[:, at_col : at_col + 128] = rows[:, i * 128 : i * 128 + 128]
+    for j in range(16):
+        place = (j // 4) * 2 + j % 2
+        cols = slice(place * 128, place * 128 + 128)
+        rhs = jnp.concatenate([r_buf[16 * core : 16 * core + 16, :, cols].reshape(256, 128) for core in range(2)], axis=1)
+        out[:, j * 256 : j * 256 + 256] = jnp.dot(pick[j], rhs, preferred_element_type=F32).astype(BF)
 
     def sent(group, ref):
         message(0, group, ref, ref, None).wait_send()
@@ -532,7 +533,7 @@
             pltpu.VMEM((4, 2, 2, 64, 1024), BF),
             pltpu.VMEM((32, 16, 1024), BF),
             pltpu.VMEM((32, 16, 1024), BF),
-            pltpu.VMEM((2, 128, 256), BF),
+            pltpu.VMEM((16, 128, 256), BF),
             pltpu.VMEM((1024, 768), F32),
             pltpu.SemaphoreType.DMA((4,)),
             pltpu.SemaphoreType.DMA((S_COUNT,)),

time: 122 us -> 120 us (0.984)
  Pallas kernels: 120 us -> 117 us
    pallas_call x1, Pallas kernels: 120 us -> 117 us  [per_device(): pl.pallas_call(kernel, out_shape=jax.ShapeDtypeStruct((128, 4096), BF), i...]
where the time goes in v5:
time: 120 us; the launch traced here: 119 us
  Pallas kernels  117 us (98%)
  local copies, waits for them, and re-layouts  2.29 us (2%)
    pallas_call x1, Pallas kernels, per_device(): pl.pallas_call(kernel, out_shape=jax.ShapeDtypeStruct((128, 4096), BF), i...  117 us

profile of v5, /device:TPU:1, one launch (start us, length us, event | category | flops | bytes accessed | tf_op | source)
XLA Modules:
  0.0 119.4 jit_solution(16818114097898044803)
XLA Ops:
  0.0 117.1 %shard_map.82 = bf16[128,4096]{1,0:T(8,128)(2,1)} custom-call(bf16[128,4096]{1,0:T(8,128)(2,1)} %tok.1, f32[1,4096]{1,0:T(1,128)} %bitcast.1, s32[1,128]{1,0:T(1,128)} %order.1, s32[1,1024]{1,0:T(1,128)} %seg.1, bf16[256,512]{1,0:T(8,128)(2,1)} %wq.1, bf16[256,512]{1,0:T(8,128)(2,1)} %wk.1, bf16[256,512]{1,0:T(8,128)(2,1)} %wv.1, bf16[512,256]{1,0:T(8,128)(2,1)} %wo.1), custom_call_target="tpu_custom_call" | custom-call | tf_op jit(solution)/shard_map/pallas_call | solution.py:515
  117.1 2.3 %copy.10 = bf16[128,4096]{1,0:T(8,128)(2,1)} copy(bf16[128,4096]{1,0:T(8,128)(2,1)} %shard_map.82) | data formatting | bytes 2097152

commit v6 on v5

--- a/solution.py
+++ b/solution.py
@@ -437,9 +437,9 @@
     farthest(1)
     gather_o.take(11)
     attend(1, zr[1])
+    attend(2, zr[-1])
     gather_o.take(7, 13, 14, 15)
     farthest(2)
-    attend(2, zr[-1])
     project_whole(1, zr[1])
     fin_message(0, 0, 1).start()
     fin_message(0, 1, 1).start()

time: 120 us -> 118 us (0.983)
  Pallas kernels: 117 us -> 115 us
    pallas_call x1, Pallas kernels: 117 us -> 115 us  [per_device(): pl.pallas_call(kernel, out_shape=jax.ShapeDtypeStruct((128, 4096), BF), i...]
where the time goes in v6:
time: 118 us; the launch traced here: 117 us
  Pallas kernels  115 us (97%)
  local copies, waits for them, and re-layouts  2.29 us (2%)
    pallas_call x1, Pallas kernels, per_device(): pl.pallas_call(kernel, out_shape=jax.ShapeDtypeStruct((128, 4096), BF), i...  115 us

profile of v6, /device:TPU:1, one launch (start us, length us, event | category | flops | bytes accessed | tf_op | source)
XLA Modules:
  0.0 117.4 jit_solution(13682230632765244011)
XLA Ops:
  0.0 115.1 %shard_map.82 = bf16[128,4096]{1,0:T(8,128)(2,1)} custom-call(bf16[128,4096]{1,0:T(8,128)(2,1)} %tok.1, f32[1,4096]{1,0:T(1,128)} %bitcast.1, s32[1,128]{1,0:T(1,128)} %order.1, s32[1,1024]{1,0:T(1,128)} %seg.1, bf16[256,512]{1,0:T(8,128)(2,1)} %wq.1, bf16[256,512]{1,0:T(8,128)(2,1)} %wk.1, bf16[256,512]{1,0:T(8,128)(2,1)} %wv.1, bf16[512,256]{1,0:T(8,128)(2,1)} %wo.1), custom_call_target="tpu_custom_call" | custom-call | tf_op jit(solution)/shard_map/pallas_call | solution.py:515
  115.1 2.3 %copy.10 = bf16[128,4096]{1,0:T(8,128)(2,1)} copy(bf16[128,4096]{1,0:T(8,128)(2,1)} %shard_map.82) | data formatting | bytes 2097152

commit v7 on v6

--- a/solution.py
+++ b/solution.py
@@ -420,6 +420,17 @@
             M_FIN + group, S_FIN, snd.at[1 + side, group, half], fin.at[group, side, half],
             z_down if side else z_up)
 
+    def project_half(i, zz, half):
+        def one(bx, carry):
+            blocks = []
+            for by in range(2):
+                first = half_of(lax.rem(bx - x + 4, 4), lax.rem(by - y + 4, 4))
+                blocks.append(bx * 4 + by + 2 * lax.rem(first + half, 2))
+            project_out(i, zz, blocks)
+            return carry
+
+        lax.fori_loop(0, 4, one, 0)
+
     def project_whole(i, zz):
         heads_of_sibling(i, zz)
 
@@ -440,12 +451,16 @@
     attend(2, zr[-1])
     gather_o.take(7, 13, 14, 15)
     farthest(2)
-    project_whole(1, zr[1])
+    heads_of_sibling(1, zr[1])
+    project_half(1, zr[1], 1)
     fin_message(0, 0, 1).start()
     fin_message(0, 1, 1).start()
-    project_whole(2, zr[-1])
+    heads_of_sibling(2, zr[-1])
+    project_half(2, zr[-1], 0)
     fin_message(1, 0, 0).start()
     fin_message(1, 1, 0).start()
+    project_half(1, zr[1], 0)
+    project_half(2, zr[-1], 1)
     message(M_OPP, S_OPP, opr, opr, None).wait_recv()
     for group in range(4):
         for side in range(2):

time: 118 us -> 118 us (level)
  no operation moved by 1% of the time
where the time goes in v7:
time: 118 us
  Pallas kernels  115 us (97%)
  local copies, waits for them, and re-layouts  2.29 us (2%)
    pallas_call x1, Pallas kernels, per_device(): pl.pallas_call(kernel, out_shape=jax.ShapeDtypeStruct((128, 4096), BF), i...  115 us

profile of v7, /device:TPU:1, one launch (start us, length us, event | category | flops | bytes accessed | tf_op | source)
XLA Modules:
  0.0 117.7 jit_solution(1396691122663317276)
XLA Ops:
  0.0 115.5 %shard_map.82 = bf16[128,4096]{1,0:T(8,128)(2,1)} custom-call(bf16[128,4096]{1,0:T(8,128)(2,1)} %tok.1, f32[1,4096]{1,0:T(1,128)} %bitcast.1, s32[1,128]{1,0:T(1,128)} %order.1, s32[1,1024]{1,0:T(1,128)} %seg.1, bf16[256,512]{1,0:T(8,128)(2,1)} %wq.1, bf16[256,512]{1,0:T(8,128)(2,1)} %wk.1, bf16[256,512]{1,0:T(8,128)(2,1)} %wv.1, bf16[512,256]{1,0:T(8,128)(2,1)} %wo.1), custom_call_target="tpu_custom_call" | custom-call | tf_op jit(solution)/shard_map/pallas_call | solution.py:530
  115.5 2.3 %copy.10 = bf16[128,4096]{1,0:T(8,128)(2,1)} copy(bf16[128,4096]{1,0:T(8,128)(2,1)} %shard_map.82) | data formatting | bytes 2097152
